TPU v7x, 256 devices: a whole 4x4x8 slice. The times are simulated.
256 devices in a mesh: dp: 4 (over x), expert: 64 (over z, y, core).
Axes of the slice: x: 4, y: 4, z: 8, core: 2. Of those that a mesh axis runs over, the one named last changes fastest.
Arguments:
- tokens: bfloat16 [4096, 4096], P(('dp', 'expert')), may hold values from -6 to 6
- cotangent: bfloat16 [4096, 4096], P(('dp', 'expert')), may hold values from -6 to 6
- gate_prob: float32 [4096, 8], P(('dp', 'expert')), may hold values from 0.05 to 0.6
- expert_ids: int32 [4096, 8], P(('dp', 'expert')), may hold values from 0 to 63, all different within a row; in each aligned block of 16 rows (0 to 15, 16 to 31, ...) at most 3 rows name the same one
- placement: int32 [64], replicated, may hold values from 0 to 63, each once
- gate_weight: bfloat16 [64, 768, 4096], P('expert', 'dp'), may hold values from -0.09375 to 0.09375
- up_weight: bfloat16 [64, 768, 4096], P('expert', 'dp'), may hold values from -0.09375 to 0.09375
- down_weight: bfloat16 [64, 768, 4096], P('expert', 'dp'), may hold values from -0.21875 to 0.21875
Outputs:
- mixed: bfloat16 [4096, 4096], P(('dp', 'expert'))
- token_grad: bfloat16 [4096, 4096], P(('dp', 'expert'))
- gate_grad: float32 [4096, 8], P(('dp', 'expert'))
- gate_weight_grad: bfloat16 [64, 768, 4096], P('expert', 'dp')
- up_weight_grad: bfloat16 [64, 768, 4096], P('expert', 'dp')
- down_weight_grad: bfloat16 [64, 768, 4096], P('expert', 'dp')
Inputs may be any that keep to these rules, and one draw needn't show every extreme that they name: `expert_ids`: in each row the 8 experts differ. In each aligned block of 16 tokens (the tokens of one device) no expert is named by more than 3 tokens, and in some blocks one is named by exactly 3. `placement`: A permutation: each slot serves exactly one expert, and no expert is replicated.
All inputs are finite; a program needn't handle non-finite values.
Results may differ from a plain program's by a relative error of at most 0.015.
Values may be sent and summed in bfloat16 or wider, within the bound.
A program may use at most 128 MiB of HBM per device.

v0:
```python
import jax
import jax.numpy as jnp
from jax import lax
from jax.sharding import PartitionSpec as P

CAP = 3


def gated(values):
    sigmoid_v = jax.nn.sigmoid(values)
    return (values * sigmoid_v, sigmoid_v * (1.0 + values * (1.0 - sigmoid_v)))


def body(tokens, cotangent, gate_prob, expert_ids, placement, gate_weight, up_weight, down_weight):
    tok_count, model_width = tokens.shape
    top_count = expert_ids.shape[1]
    expert_devs = lax.axis_size("expert")
    local_experts = gate_weight.shape[0]
    total_experts = placement.shape[0]
    capacity = CAP
    flat_ids = expert_ids.reshape(-1)
    matches_id = flat_ids[:, None] == jnp.arange(total_experts, dtype=jnp.int32)[None, :]
    slot_ids = jnp.sum(jnp.where(matches_id, placement[None, :], 0), axis=1)
    pair_order = jnp.arange(flat_ids.shape[0], dtype=jnp.int32)
    earlier = (slot_ids[:, None] == slot_ids[None, :]) & (pair_order[None, :] < pair_order[:, None])
    position = slot_ids * capacity + jnp.sum(earlier.astype(jnp.int32), axis=1)
    matches = jnp.arange(total_experts * capacity, dtype=jnp.int32)[:, None] == position[None, :]
    matches = matches.reshape(total_experts * capacity, tok_count, top_count)
    dispatch = jnp.any(matches, axis=2).astype(jnp.bfloat16)
    weight_map = jnp.sum(jnp.where(matches, gate_prob[None, :, :], 0.0), axis=2)
    sent_rows = jnp.dot(dispatch, tokens, preferred_element_type=jnp.float32).astype(jnp.bfloat16)
    sent_grads = jnp.dot(
        weight_map, cotangent.astype(jnp.float32), precision=lax.Precision.HIGHEST
    ).astype(jnp.bfloat16)
    block_shape = (1, expert_devs, local_experts, capacity, model_width)
    sent_rows = sent_rows.reshape(block_shape)
    sent_grads = sent_grads.reshape(block_shape)
    got_rows, got_grads = (
        lax.all_to_all(sent_rows, "expert", split_axis=1, concat_axis=1, tiled=True),
        lax.all_to_all(sent_grads, "expert", split_axis=1, concat_axis=1, tiled=True),
    )
    routed, routed_grads = (
        lax.all_gather(got_rows, "dp", axis=0, tiled=True),
        lax.all_gather(got_grads, "dp", axis=0, tiled=True),
    )
    gate_pre = jnp.einsum(
        "asjcd,jfd->asjcf", routed, gate_weight, preferred_element_type=jnp.float32
    )
    up_pre = jnp.einsum("asjcd,jfd->asjcf", routed, up_weight, preferred_element_type=jnp.float32)
    silu_v, slope = gated(gate_pre)
    hidden = (silu_v * up_pre).astype(jnp.bfloat16)
    out_part = jnp.einsum(
        "asjcf,jfd->asjcd", hidden, down_weight, preferred_element_type=jnp.float32
    )
    d_hidden = jnp.einsum(
        "asjcd,jfd->asjcf", routed_grads, down_weight, preferred_element_type=jnp.float32
    )
    d_gate_pre = (d_hidden * up_pre * slope).astype(jnp.bfloat16)
    d_up_pre = (d_hidden * silu_v).astype(jnp.bfloat16)
    back_part = jnp.einsum(
        "asjcf,jfd->asjcd", d_gate_pre, gate_weight, preferred_element_type=jnp.float32
    )
    back_part = back_part + jnp.einsum(
        "asjcf,jfd->asjcd", d_up_pre, up_weight, preferred_element_type=jnp.float32
    )
    down_grad = jnp.einsum(
        "asjcf,asjcd->jfd", hidden, routed_grads, preferred_element_type=jnp.float32
    ).astype(jnp.bfloat16)
    gate_grad_w = jnp.einsum(
        "asjcf,asjcd->jfd", d_gate_pre, routed, preferred_element_type=jnp.float32
    ).astype(jnp.bfloat16)
    up_grad_w = jnp.einsum(
        "asjcf,asjcd->jfd", d_up_pre, routed, preferred_element_type=jnp.float32
    ).astype(jnp.bfloat16)
    summed = (
        lax.psum_scatter(
            out_part.astype(jnp.bfloat16), "dp", scatter_dimension=0, tiled=True
        ).astype(jnp.float32),
        lax.psum_scatter(
            back_part.astype(jnp.bfloat16), "dp", scatter_dimension=0, tiled=True
        ).astype(jnp.float32),
    )
    back_out, back_grad = (
        lax.all_to_all(
            summed[0].astype(jnp.bfloat16), "expert", split_axis=1, concat_axis=1, tiled=True
        ),
        lax.all_to_all(
            summed[1].astype(jnp.bfloat16), "expert", split_axis=1, concat_axis=1, tiled=True
        ),
    )
    out_flat = back_out.reshape(total_experts * capacity, model_width)
    grad_flat = back_grad.reshape(total_experts * capacity, model_width)
    chosen_out = out_flat[position].reshape(tok_count, top_count, model_width)
    chosen_grad = grad_flat[position].reshape(tok_count, top_count, model_width)
    mixed = jnp.einsum(
        "tk,tkd->td", gate_prob, chosen_out.astype(jnp.float32), precision=lax.Precision.HIGHEST
    ).astype(jnp.bfloat16)
    gate_grad = jnp.einsum("td,tkd->tk", cotangent, chosen_out, preferred_element_type=jnp.float32)
    token_grad = jnp.sum(chosen_grad.astype(jnp.float32), axis=1).astype(jnp.bfloat16)
    return (mixed, token_grad, gate_grad, gate_grad_w, up_grad_w, down_grad)


def solution(mesh):
    return jax.shard_map(
        body,
        mesh=mesh,
        in_specs=(
            P(("dp", "expert"), None),
            P(("dp", "expert"), None),
            P(("dp", "expert"), None),
            P(("dp", "expert"), None),
            P(),
            P("expert", "dp", None),
            P("expert", "dp", None),
            P("expert", "dp", None),
        ),
        out_specs=(
            P(("dp", "expert"), None),
            P(("dp", "expert"), None),
            P(("dp", "expert"), None),
            P("expert", "dp", None),
            P("expert", "dp", None),
            P("expert", "dp", None),
        ),
        check_vma=False,
    )
```

profile of v0, /device:TPU:1, one launch (start us, length us, event | category | flops | bytes accessed | tf_op | source)
XLA Modules:
  0.0 441.2 jit_solution(17022439714475222526)
XLA Ops:
  7.2 0.0 all-gather.3.cloned.1.call-start
  7.2 0.9 copy.32
  8.1 0.1 eq.43
  8.2 0.7 select_reduce_fusion.1
  8.9 0.2 convert_reduce_fusion
  9.1 0.1 add.48
  9.2 0.1 fusion.73
  9.3 1.5 convolution_convert_fusion.2
  10.9 2.3 reshape.130
  13.2 62.8 %all_to_all.20 = bf16[1,64,1,3,4096]{4,3,0,2,1:T(4,128)(2,1)S(1)} all-to-all(bf16[1,64,1,3,4096]{4,3,0,2,1:T(4,128)(2,1)} %bitcast.180), channel_id=1, replica_groups=mesh['dp'=4,'expert'=64] {'expert'}, dimensions={1} | all-to-all | bytes 3145728 | tf_op jit(solution)/shard_map/all_to_all | solution.py:39
  76.0 2.3 copy.34
  78.3 0.0 all-gather.5.cloned.1.call-start
  78.4 0.1 copy.36
  78.5 0.1 select_reduce_fusion
  78.6 1.4 convolution_convert_fusion.1
  80.1 2.4 reshape.138
  82.4 56.7 %all_to_all.21 = bf16[1,64,1,3,4096]{4,3,0,2,1:T(4,128)(2,1)S(1)} all-to-all(bf16[1,64,1,3,4096]{4,3,0,2,1:T(4,128)(2,1)} %bitcast.181), channel_id=1, replica_groups=mesh['dp'=4,'expert'=64] {'expert'}, dimensions={1} | all-to-all | bytes 3145728 | tf_op jit(solution)/shard_map/all_to_all | solution.py:40
  139.1 2.3 copy.38
  141.4 0.2 reduce-scatter.3.cloned.1.call-start
  141.7 2.7 all-gather.3.cloned.1.call-done
  144.4 6.1 %fusion.53 = f32[4,64,1,3,192]{4,1,3,0,2:T(8,128)} fusion(bf16[1,192,4096]{2,1,0:T(8,128)(2,1)} %param.14, bf16[4,64,1,3,4096]{4,1,3,2,0:T(8,128)(2,1)} %all-gather.3.cloned.1.call-done), kind=kOutput, calls=%fused_computation.37 | convolution fusion | flops 1207959552 | bytes 8454144 | tf_op jit(solution)/shard_map/asjcd,jfd->asjcf/dot_general | solution.py:49
  150.4 2.8 fusion.48
  153.2 62.5 %all-gather.5.cloned.1.call-done = bf16[4,64,1,3,4096]{4,1,3,2,0:T(8,128)(2,1)} async-done(((bf16[1,64,1,3,4096]{4,1,3,2,0:T(8,128)(2,1)}), bf16[4,64,1,3,4096]{4,1,3,2,0:T(8,128)(2,1)}) %all-gather.5.cloned.1.call-update) | async-done | bytes 6291472 | tf_op jit(solution)/shard_map/all_gather | solution.py:44
  215.7 6.0 %fusion.69 = (bf16[4,64,3,192]{3,1,2,0:T(8,128)(2,1)}, bf16[4,64,1,3,192]{4,1,3,0,2:T(8,128)(2,1)}, bf16[4,64,3,192]{3,1,2,0:T(8,128)(2,1)S(1)}) fusion(f32[4,64,1,3,192]{4,1,3,0,2:T(8,128)} %fusion.48, f32[4,64,1,3,192]{4,1,3,0,2:T(8,128)} %fusion.53, bf16[1,192,4096]{2,1,0:T(8,128)(2,1)S(1)} %copy-done, ...), kind=kOutput, calls=%fused_computation.50 | convolution fusion | flops 1210171392 | bytes 9928704 | tf_op jit(solution)/shard_map/asjcd,jfd->asjcf/dot_general | solution.py:55
  221.7 4.4 fusion.12
  226.1 0.3 reduce-scatter.5.cloned.1.call-start
  226.4 2.9 fusion.43
  229.4 4.4 %fusion.13 = bf16[4,64,1,3,4096]{4,1,3,0,2:T(8,128)(2,1)} fusion(f32[4,64,3,4096]{3,1,2,0:T(8,128)S(1)} %fusion.43, bf16[4,64,3,192]{3,1,2,0:T(8,128)(2,1)S(1)} %copy-done.6, bf16[1,192,4096]{2,1,0:T(8,128)(2,1)S(1)} %copy-done.4), kind=kOutput, calls=%fused_computation.17 | convolution fusion | flops 1214251008 | bytes 20742144 | tf_op jit(solution)/shard_map/asjcf,jfd->asjcd/dot_general | solution.py:63
  233.9 59.7 %reduce-scatter.3.cloned.1.call-done = bf16[1,64,1,3,4096]{4,1,3,0,2:T(8,128)(2,1)} async-done(((bf16[4,64,1,3,4096]{4,1,3,0,2:T(8,128)(2,1)}), bf16[1,64,1,3,4096]{4,1,3,0,2:T(8,128)(2,1)}) %reduce-scatter.3.cloned.1.call-update) | async-done | bytes 1572880 | tf_op jit(solution)/shard_map/reduce_scatter | solution.py:76
  293.6 4.1 copy.35
  297.6 10.8 %all-to-all-start.1 = ((bf16[1,64,1,3,4096]{4,3,0,2,1:T(4,128)(2,1)}), bf16[1,64,1,3,4096]{4,3,0,2,1:T(4,128)(2,1)}, u32[]{:S(2)}, u32[]{:S(2)}) async-start(bf16[1,64,1,3,4096]{4,3,0,2,1:T(4,128)(2,1)} %copy.35), calls=%async_computation.2 | async-start | bytes 4194304 | tf_op jit(solution)/shard_map/all_to_all | solution.py:84
  308.5 53.8 %reduce-scatter.5.cloned.1.call-done = bf16[1,64,1,3,4096]{4,1,3,0,2:T(8,128)(2,1)} async-done(((bf16[4,64,1,3,4096]{4,1,3,0,2:T(8,128)(2,1)}), bf16[1,64,1,3,4096]{4,1,3,0,2:T(8,128)(2,1)}) %reduce-scatter.5.cloned.1.call-update) | async-done | bytes 1572880 | tf_op jit(solution)/shard_map/reduce_scatter | solution.py:79
  362.3 4.1 copy.39
  366.3 10.9 %all-to-all-start.3 = ((bf16[1,64,1,3,4096]{4,3,0,2,1:T(4,128)(2,1)}), bf16[1,64,1,3,4096]{4,3,0,2,1:T(4,128)(2,1)}, u32[]{:S(2)}, u32[]{:S(2)}) async-start(bf16[1,64,1,3,4096]{4,3,0,2,1:T(4,128)(2,1)} %copy.39), calls=%async_computation.5 | async-start | bytes 4194304 | tf_op jit(solution)/shard_map/all_to_all | solution.py:87
  377.2 0.1 copy.43
  377.3 5.5 %fusion.38 = bf16[1,192,4096]{2,1,0:T(8,128)(2,1)} fusion(bf16[4,64,3,192]{3,1,2,0:T(8,128)(2,1)S(1)} %get-tuple-element.10, bf16[4,64,1,3,4096]{4,1,3,2,0:T(8,128)(2,1)} %all-gather.5.cloned.1.call-done), kind=kOutput, calls=%fused_computation.28 | convolution fusion | flops 1208745984 | bytes 8159232 | tf_op jit(solution)/shard_map/asjcf,asjcd->jfd/dot_general | solution.py:66
  382.8 5.5 %fusion.35 = bf16[1,192,4096]{2,1,0:T(8,128)(2,1)} fusion(bf16[4,64,3,192]{3,1,2,0:T(8,128)(2,1)S(1)} %copy-done.7, bf16[4,64,1,3,4096]{4,1,3,2,0:T(8,128)(2,1)} %all-gather.3.cloned.1.call-done), kind=kOutput, calls=%fused_computation.27 | convolution fusion | flops 1208745984 | bytes 8159232 | tf_op jit(solution)/shard_map/asjcf,asjcd->jfd/dot_general | solution.py:72
  388.3 2.6 fusion.32
  391.0 3.1 reshape.136
  394.1 1.2 gather_fusion
  395.3 1.0 fusion.65
  396.3 0.8 copy.53
  397.1 0.8 fusion.63
  397.9 0.7 copy.46
  398.6 28.2 %all-to-all-done.3 = bf16[1,64,1,3,4096]{4,3,0,2,1:T(4,128)(2,1)} async-done(((bf16[1,64,1,3,4096]{4,3,0,2,1:T(4,128)(2,1)}), bf16[1,64,1,3,4096]{4,3,0,2,1:T(4,128)(2,1)}, u32[]{:S(2)}, u32[]{:S(2)}) %all-to-all-start.3) | async-done | bytes 1572896 | tf_op jit(solution)/shard_map/all_to_all | solution.py:87
  426.8 3.1 reshape.142
  429.9 2.2 gather_fusion.1
  432.1 2.6 bitcast_reduce_fusion
  (34 shorter events, 0.2 us)
Async XLA Ops:
  7.2 208.5 %copy-start = (bf16[1,192,4096]{2,1,0:T(8,128)(2,1)S(1)}, bf16[1,192,4096]{2,1,0:T(8,128)(2,1)}, u32[]{:S(2)}) copy-start(bf16[1,192,4096]{2,1,0:T(8,128)(2,1)} %param.15) | copy-start | bytes 4718596
  7.2 137.2 %all-gather.3.cloned.1.call-start = ((), (), s32[]{:S(2)}) async-start(), calls=%async_computation.6 | async-start | bytes 7864320 | tf_op jit(solution)/shard_map/all_gather | solution.py:43
  76.0 2.4 copy-start.10
  76.0 2.6 copy-start.8
  78.3 137.3 %all-gather.5.cloned.1.call-start = ((), (), s32[]{:S(2)}) async-start(), calls=%async_computation.8 | async-start | bytes 7864320 | tf_op jit(solution)/shard_map/all_gather | solution.py:44
  141.4 9.0 %copy-start.3 = (bf16[1,192,4096]{2,1,0:T(8,128)(2,1)S(1)}, bf16[1,192,4096]{2,1,0:T(8,128)(2,1)}, u32[]{:S(2)}) copy-start(bf16[1,192,4096]{2,1,0:T(8,128)(2,1)} %param.13) | copy-start | bytes 4718596
  141.4 152.1 %reduce-scatter.3.cloned.1.call-start = ((), (), s32[]{:S(2)}) async-start(), calls=%async_computation.7 | async-start | bytes 7864320 | tf_op jit(solution)/shard_map/reduce_scatter | solution.py:76
  144.4 6.1 %copy-start.2 = (bf16[4,64,1,3,4096]{4,1,3,2,0:T(8,128)(2,1)S(1)}, bf16[4,64,1,3,4096]{4,1,3,2,0:T(8,128)(2,1)}, u32[]{:S(2)}) copy-start(bf16[4,64,1,3,4096]{4,1,3,2,0:T(8,128)(2,1)} %all-gather.3.cloned.1.call-done) | copy-start | bytes 18874372
  226.1 136.1 %reduce-scatter.5.cloned.1.call-start = ((), (), s32[]{:S(2)}) async-start(), calls=%async_computation.9 | async-start | bytes 7864320 | tf_op jit(solution)/shard_map/reduce_scatter | solution.py:79
  226.4 3.0 copy-start.4
  226.4 3.0 copy-start.6
  297.6 68.7 %all-to-all-start.1 = ((bf16[1,64,1,3,4096]{4,3,0,2,1:T(4,128)(2,1)}), bf16[1,64,1,3,4096]{4,3,0,2,1:T(4,128)(2,1)}, u32[]{:S(2)}, u32[]{:S(2)}) async-start(bf16[1,64,1,3,4096]{4,3,0,2,1:T(4,128)(2,1)} %copy.35), calls=%async_computation.2 | async-start | bytes 4194304 | tf_op jit(solution)/shard_map/all_to_all | solution.py:84
  366.3 60.4 %all-to-all-start.3 = ((bf16[1,64,1,3,4096]{4,3,0,2,1:T(4,128)(2,1)}), bf16[1,64,1,3,4096]{4,3,0,2,1:T(4,128)(2,1)}, u32[]{:S(2)}, u32[]{:S(2)}) async-start(bf16[1,64,1,3,4096]{4,3,0,2,1:T(4,128)(2,1)} %copy.39), calls=%async_computation.5 | async-start | bytes 4194304 | tf_op jit(solution)/shard_map/all_to_all | solution.py:87
  377.3 5.5 %copy-start.7 = (bf16[4,64,3,192]{3,1,2,0:T(8,128)(2,1)S(1)}, bf16[4,64,3,192]{3,1,2,0:T(8,128)(2,1)}, u32[]{:S(2)}) copy-start(bf16[4,64,3,192]{3,1,2,0:T(8,128)(2,1)} %get-tuple-element.8) | copy-start | bytes 884740
  377.3 11.0 %slice-start = ((s8[6291456]{0:T(1024)(128)(4,1)}), s8[4194304]{0:T(1024)(128)(4,1)S(1)}, s32[]{:S(2)}) async-start(s8[6291456]{0:T(1024)(128)(4,1)} %bitcast.178), calls=%async_computation.10 | async-start | bytes 8388608
  382.8 5.5 %slice-start.1 = ((s8[6291456]{0:T(1024)(128)(4,1)}), s8[2097152]{0:T(1024)(128)(4,1)S(1)}, s32[]{:S(2)}) async-start(s8[6291456]{0:T(1024)(128)(4,1)} %bitcast.178), calls=%async_computation.11 | async-start | bytes 4194304
  382.8 5.5 %copy-start.5 = (bf16[4,64,1,3,192]{4,1,3,0,2:T(8,128)(2,1)S(1)}, bf16[4,64,1,3,192]{4,1,3,0,2:T(8,128)(2,1)}, u32[]{:S(2)}) copy-start(bf16[4,64,1,3,192]{4,1,3,0,2:T(8,128)(2,1)} %get-tuple-element.9) | copy-start | bytes 884740
  394.1 3.0 copy-start.9
  429.9 4.8 %copy-start.1 = (bf16[1,192,4096]{2,1,0:T(8,128)(2,1)S(1)}, bf16[1,192,4096]{2,1,0:T(8,128)(2,1)}, u32[]{:S(2)}) copy-start(bf16[1,192,4096]{2,1,0:T(8,128)(2,1)} %param.15) | copy-start | bytes 4718596
Sparse Core Ops, SparseCore 0:
  78.5 65.8 all-gather.2
  146.7 68.9 all-gather.4
  226.3 67.2 reduce-scatter.2
  296.0 66.2 reduce-scatter.4
where the time goes:
time: 443 us; the launch traced here: 441 us
  waiting for transfers between devices  207 us (47%)
  blocking collectives  120 us (27%)
  matrix products  45 us (10%)
  local copies, waits for them, and re-layouts  29.8 us (7%)
  starting transfers between devices  22.3 us (5%)
  between operations  14 us (3%)
    all_to_all x1, blocking collectives, body(): lax.all_to_all(sent_rows, 'expert', split_axis=1, concat_axis=1, tiled=True)  62.8 us
    all_gather x1, waiting for transfers between devices, body(): lax.all_gather(got_grads, 'dp', axis=0, tiled=True)  62.5 us
    reduce_scatter x1, waiting for transfers between devices, body(): lax.psum_scatter(out_part.astype(jnp.bfloat16), 'dp', scatter_dimension=0...  59.7 us
    all_to_all x1, blocking collectives, body(): lax.all_to_all(sent_grads, 'expert', split_axis=1, concat_axis=1, tiled=T...  56.7 us
    reduce_scatter x1, waiting for transfers between devices, body(): lax.psum_scatter(back_part.astype(jnp.bfloat16), 'dp', scatter_dimension=...  53.8 us
    all_to_all x1, waiting for transfers between devices, body(): lax.all_to_all(summed[1].astype(jnp.bfloat16), 'expert', split_axis=1, co...  28.2 us
    all_to_all x1, starting transfers between devices, body(): lax.all_to_all(summed[1].astype(jnp.bfloat16), 'expert', split_axis=1, co...  10.9 us
    all_to_all x1, starting transfers between devices, body(): lax.all_to_all(summed[0].astype(jnp.bfloat16), 'expert', split_axis=1, co...  10.8 us
  transfers between devices with their start and end apart: 6, of which 5 were waited for; matrix products, arithmetic and copies ran while one was open for 12% of the time, Pallas kernels for 0%

commit v1 on v0

v1 whole, which is shorter than its diff:
```python
import jax
import jax.numpy as jnp
from jax import lax
from jax.experimental import pallas as pl
from jax.experimental.pallas import tpu as pltpu
from jax.sharding import PartitionSpec as P

CAP = 3
NX, NZ, NY, NC = 4, 8, 4, 2
MESH = pl.DeviceIdType.MESH
F32, BF16 = jnp.float32, jnp.bfloat16

TOK = 16
BLOCKS = NC * NZ
GROUP = BLOCKS * TOK
ROWS_J = BLOCKS * CAP
ROWS = NY * ROWS_J
CW = 512
SLOTS = 4


def nt(a, b):
    return lax.dot_general(a, b, (((1,), (1,)), ((), ())), preferred_element_type=F32)


def nn(a, b):
    return jnp.dot(a, b, preferred_element_type=F32)


def split3(v):
    a = v.astype(BF16)
    rest = v - a.astype(F32)
    b = rest.astype(BF16)
    return a, b, (rest - b.astype(F32)).astype(BF16)


def iota(shape, dim):
    return lax.broadcasted_iota(jnp.int32, shape, dim)


def row_parts(r):
    q = r >> 4
    j = (q >= 3).astype(jnp.int32) + (q >= 6).astype(jnp.int32) + (q >= 9).astype(jnp.int32)
    return j, q - 3 * j, r & 15


def kernel(
    x_hbm, c_hbm, p_ref, ids_ref, place_ref, wg_hbm, wu_hbm, wd_hbm,
    mixed_ref, tgrad_ref, ggrad_ref, dwg_hbm, dwu_hbm, dwd_hbm,
    zbuf, sbuf, xr, wg, wu, wd, pb, rly, fin_a, fin_b, yr, cs, cr, zs, zr, outf,
    g_acc, u_acc, d_acc, hid, dgp, dup, hid_t, dgp_t, dup_t, stage,
    meta, dmat, dmat_t, w1, w2, prow, gacc, gsend, grecv, gz_s, gz_r,
    load_sem, bar_unused,
    zss, zrs, ess, ers, yss, yrs, xss, xrs,
    bxss, bxrs, byss, byrs, bess, bers, bzss, bzrs,
    mzss, mzrs, mess, mers, gess, gers, gzss, gzrs, wsem,
):
    D = x_hbm.shape[1]
    FQ = wg_hbm.shape[0]
    NH = D // CW
    N = 2 * NH
    x = lax.axis_index("dp")
    e = lax.axis_index("expert")
    z, y, c = e // (NY * NC), (e // NC) % NY, e % NC
    right, left, opp = (x + 1) % NX, (x + 3) % NX, (x + 2) % NX

    def at_z(i):
        return {"expert": (((z + i) % NZ) * NY + y) * NC + c}

    def at_y(i):
        return {"expert": (z * NY + (y + i) % NY) * NC + c}

    other = {"expert": (z * NY + y) * NC + (1 - c)}

    def cols(k):
        return pl.ds(pl.multiple_of(k * CW, CW), CW)

    def rows(start, size):
        return pl.ds(pl.multiple_of(start, 16), size)

    def remote(src, dst, ss, rs, dev):
        return pltpu.make_async_remote_copy(
            src_ref=src, dst_ref=dst, send_sem=ss, recv_sem=rs, device_id=dev, device_id_type=MESH
        )

    mine = rows((c * NZ + z) * TOK, TOK)
    loads = [
        pltpu.make_async_copy(x_hbm, zbuf.at[mine, pl.ds(0, D)], load_sem.at[0]),
        pltpu.make_async_copy(c_hbm, zbuf.at[mine, pl.ds(D, D)], load_sem.at[1]),
        pltpu.make_async_copy(wg_hbm, wg, load_sem.at[2]),
        pltpu.make_async_copy(wu_hbm, wu, load_sem.at[3]),
        pltpu.make_async_copy(wd_hbm, wd, load_sem.at[4]),
    ]
    for cp in loads:
        cp.start()
    barrier = pltpu.get_barrier_semaphore()
    peers = [at_z(i) for i in range(1, NZ)] + [at_y(i) for i in range(1, NY)]
    peers += [other, {"dp": right}, {"dp": left}]
    for dev in peers:
        pl.semaphore_signal(barrier, inc=1, device_id=dev, device_id_type=MESH)

    ids = ids_ref[...]
    probs = p_ref[...]
    place = place_ref[...].astype(F32)
    lane64 = iota((TOK, place.shape[1]), 1)
    lane = iota((TOK, 128), 1)
    own = jnp.zeros((TOK, 128), F32)
    for k in range(8):
        slot = jnp.sum(jnp.where(ids[:, k : k + 1] == lane64, place, 0.0), axis=1, keepdims=True)
        own = jnp.where(lane == k, slot, own)
        own = jnp.where(lane == 8 + k, probs[:, k : k + 1], own)
    meta[mine, :] = own
    loads[0].wait()
    loads[1].wait()
    pl.semaphore_wait(barrier, len(peers))

    def z_copy(i, k):
        part = (mine, cols(k))
        return remote(zbuf.at[part], zbuf.at[part], zss.at[i - 1, k], zrs.at[i - 1, k], at_z(i))

    def z_wait(i, k):
        part = (rows((c * NZ + (z + NZ - i) % NZ) * TOK, TOK), cols(k))
        remote(zbuf.at[part], zbuf.at[part], zss.at[i - 1, k], zrs.at[i - 1, k], at_z(i)).wait_recv()

    def e_copy(k):
        part = (rows(c * NZ * TOK, NZ * TOK), cols(k))
        return remote(zbuf.at[part], zbuf.at[part], ess.at[k], ers.at[k], other)

    def e_wait(k):
        part = (rows((1 - c) * NZ * TOK, NZ * TOK), cols(k))
        remote(zbuf.at[part], zbuf.at[part], ess.at[k], ers.at[k], other).wait_recv()

    def y_copy(i, k):
        src = sbuf.at[rows(((y + i) % NY) * ROWS_J, ROWS_J), cols(k)]
        dst = xr.at[rows(x * ROWS + y * ROWS_J, ROWS_J), cols(k)]
        return remote(src, dst, yss.at[i - 1, k], yrs.at[i - 1, k], at_y(i))

    def y_wait(i, k):
        dst = xr.at[rows(x * ROWS + ((y + NY - i) % NY) * ROWS_J, ROWS_J), cols(k)]
        remote(dst, dst, yss.at[i - 1, k], yrs.at[i - 1, k], at_y(i)).wait_recv()

    def block(b):
        return rows(b * ROWS, ROWS)

    def x_copy(d, k):
        if d == 2:
            par = k % 2
            ref = xr.at[block((x + 3 - 2 * par) % NX), cols(k)]
            dev = {"dp": (x + 1 + 2 * par) % NX}
        else:
            ref = xr.at[block(x), cols(k)]
            dev = {"dp": left if d else right}
        return remote(ref, ref, xss.at[d, k], xrs.at[d, k], dev)

    def x_wait(d, k):
        ref = xr.at[block((left, right, opp)[d]), cols(k)]
        remote(ref, ref, xss.at[d, k], xrs.at[d, k], {"dp": right}).wait_recv()

    def slot_of(k, b):
        return pb.at[k % SLOTS, block(b)]

    def bx_copy(d, k):
        par = k % 2
        rdev, ddev = (x + 3 - 2 * par) % NX, (x + 1 + 2 * par) % NX
        if d == 0:
            src, dst, dev = slot_of(k, opp), rly.at[:, cols(k)], rdev
        elif d == 1:
            src, dst, dev = slot_of(k, rdev), fin_b.at[:, cols(k)], rdev
        else:
            src, dst, dev = slot_of(k, ddev), fin_a.at[:, cols(k)], ddev
        return remote(src, dst, bxss.at[d, k], bxrs.at[d, k], {"dp": dev})

    def by_copy(i, k):
        src = sbuf.at[rows(((y + i) % NY) * ROWS_J, ROWS_J), cols(k)]
        dst = yr.at[rows(y * ROWS_J, ROWS_J), cols(k)]
        return remote(src, dst, byss.at[i - 1, k], byrs.at[i - 1, k], at_y(i))

    def by_wait(i, k):
        dst = yr.at[rows(((y + NY - i) % NY) * ROWS_J, ROWS_J), cols(k)]
        remote(dst, dst, byss.at[i - 1, k], byrs.at[i - 1, k], at_y(i)).wait_recv()

    def be_copy(k):
        return remote(cs.at[:, cols(k)], cr.at[:, cols(k)], bess.at[k], bers.at[k], other)

    def bz_copy(i, k):
        src = zs.at[rows(((z + i) % NZ) * TOK, TOK), cols(k)]
        dst = zr.at[rows(z * TOK, TOK), cols(k)]
        return remote(src, dst, bzss.at[i - 1, k], bzrs.at[i - 1, k], at_z(i))

    def bz_wait(i, k):
        dst = zr.at[rows(((z + NZ - i) % NZ) * TOK, TOK), cols(k)]
        remote(dst, dst, bzss.at[i - 1, k], bzrs.at[i - 1, k], at_z(i)).wait_recv()

    def mz_copy(i):
        return remote(meta.at[mine], meta.at[mine], mzss.at[i - 1], mzrs.at[i - 1], at_z(i))

    me_part = rows(c * NZ * TOK, NZ * TOK)
    oth_part = rows((1 - c) * NZ * TOK, NZ * TOK)
    me_copy = remote(meta.at[me_part], meta.at[me_part], mess, mers, other)

    for i in range(1, NZ):
        mz_copy(i).start()

    def st_a(k):
        for i in (1, 7, 2, 6, 3, 5, 4):
            z_copy(i, k).start()

    st_a(0)
    st_a(1)
    for i in range(1, NZ):
        part = rows((c * NZ + (z + NZ - i) % NZ) * TOK, TOK)
        remote(meta.at[part], meta.at[part], mzss.at[i - 1], mzrs.at[i - 1], at_z(i)).wait_recv()
    me_copy.start()
    remote(meta.at[oth_part], meta.at[oth_part], mess, mers, other).wait_recv()

    info = meta[...]
    lane = iota((GROUP, 128), 1)
    target = jnp.where(lane < NY, z * (NY * NC) + c + NC * lane, -1).astype(F32)
    used = jnp.zeros((GROUP, 128), F32)
    prob = jnp.zeros((GROUP, 128), F32)
    for k in range(8):
        hit = info[:, k : k + 1] == target
        used += jnp.where(hit, 1.0, 0.0)
        prob += jnp.where(hit, info[:, 8 + k : 9 + k], 0.0)
    t_row, t_col = iota((GROUP, GROUP), 0), iota((GROUP, GROUP), 1)
    before = ((t_row >> 4) == (t_col >> 4)) & (t_col < t_row)
    used_b = used.astype(BF16)
    rank_b = nn(jnp.where(before, 1.0, 0.0).astype(BF16), used_b).astype(BF16)
    probs3 = split3(prob)
    rj, rrank, rblk = row_parts(iota((ROWS, 128), 0))
    spread = jnp.where(rj == iota((ROWS, 128), 1), 1.0, 0.0).astype(BF16)
    rj, rrank, rblk = row_parts(iota((ROWS, GROUP), 0))
    keep = (rblk == (iota((ROWS, GROUP), 1) >> 4)) & (nt(spread, rank_b) == rrank.astype(F32))
    d_f = jnp.where(keep, nt(spread, used_b), 0.0)
    dmat[...] = d_f.astype(BF16)
    weight = nt(spread, probs3[0]) + nt(spread, probs3[1]) + nt(spread, probs3[2])
    prow[...] = jnp.broadcast_to(jnp.sum(d_f * weight, axis=1, keepdims=True), prow.shape)
    rj, rrank, rblk = row_parts(iota((128, ROWS), 1))
    spread_t = jnp.where(rj == iota((128, ROWS), 0), 1.0, 0.0).astype(BF16)
    rj, rrank, rblk = row_parts(iota((GROUP, ROWS), 1))
    keep = (rblk == (iota((GROUP, ROWS), 0) >> 4)) & (nn(rank_b, spread_t) == rrank.astype(F32))
    d_t = jnp.where(keep, nn(used_b, spread_t), 0.0)
    dmat_t[...] = d_t.astype(BF16)
    weight = nn(probs3[0], spread_t) + nn(probs3[1], spread_t) + nn(probs3[2], spread_t)
    weight = d_t * weight
    w1[...] = weight.astype(BF16)
    w2[...] = (weight - weight.astype(BF16).astype(F32)).astype(BF16)

    g_acc[...] = jnp.zeros_like(g_acc)
    u_acc[...] = jnp.zeros_like(u_acc)
    d_acc[...] = jnp.zeros_like(d_acc)
    gacc[...] = jnp.zeros_like(gacc)
    loads[2].wait()
    loads[3].wait()
    loads[4].wait()

    def st_b(k):
        for i in range(1, NZ):
            z_wait(i, k)
        e_copy(k).start()

    def st_c(k):
        e_wait(k)
        scale = jnp.where(k < NH, 1.0, prow[:, 0:1])
        sbuf[:, cols(k)] = (nn(dmat[...], zbuf[:, cols(k)]) * scale).astype(BF16)
        for i in range(1, NY):
            y_copy(i, k).start()
        xr[rows(x * ROWS + y * ROWS_J, ROWS_J), cols(k)] = sbuf[rows(y * ROWS_J, ROWS_J), cols(k)]

    def st_d(k):
        for i in range(1, NY):
            y_wait(i, k)
        x_copy(0, k).start()
        x_copy(1, k).start()

    def st_e(k):
        x_wait(0, k)
        x_wait(1, k)
        x_copy(2, k).start()

    def st_f(k):
        x_wait(2, k)

        @pl.when(k < NH)
        def _():
            part = xr[:, cols(k)]
            g_acc[...] += nt(part, wg[:, cols(k)])
            u_acc[...] += nt(part, wu[:, cols(k)])

        @pl.when(k >= NH)
        def _():
            d_acc[...] += nt(xr[:, cols(k)], wd[:, cols(k - NH)])

        @pl.when(k == NH - 1)
        def _():
            def one(i, carry):
                part = rows(i * 64, 64)
                g, u = g_acc[part, :], u_acc[part, :]
                sig = 1.0 / (1.0 + jnp.exp(-g))
                silu = g * sig
                hid[part, :] = (silu * u).astype(BF16)
                g_acc[part, :] = u * (sig * (1.0 + g * (1.0 - sig)))
                u_acc[part, :] = silu
                return carry

            lax.fori_loop(0, NX * ROWS // 64, one, 0)
            hid_t[...] = hid[...].astype(F32).T.astype(BF16)

        @pl.when(k == N - 1)
        def _():
            def one(i, carry):
                part = rows(i * 64, 64)
                dh = d_acc[part, :]
                dgp[part, :] = (dh * g_acc[part, :]).astype(BF16)
                dup[part, :] = (dh * u_acc[part, :]).astype(BF16)
                return carry

            lax.fori_loop(0, NX * ROWS // 64, one, 0)

    def st_g(k):
        for i in range(1, NZ):
            z_copy(i, k).wait_send()
        e_copy(k).wait_send()
        for i in range(1, NY):
            y_copy(i, k).wait_send()
        for d in range(3):
            x_copy(d, k).wait_send()

    def st_w(k):
        for d in range(3):
            bx_copy(d, k).wait_send()

    def st_p(k):
        @pl.when(k < NH)
        def _():
            pb[k % SLOTS] = nn(hid[...], wd[:, cols(k)]).astype(BF16)

        @pl.when(k >= NH)
        def _():
            part = cols(k - NH)
            pb[k % SLOTS] = (nn(dgp[...], wg[:, part]) + nn(dup[...], wu[:, part])).astype(BF16)

        bx_copy(0, k).start()
        bx_copy(2, k).start()

    def st_q(k):
        bx_copy(0, k).wait_recv()
        ref = slot_of(k, (x + 3 - 2 * (k % 2)) % NX)
        ref[...] = (rly[:, cols(k)].astype(F32) + ref[...].astype(F32)).astype(BF16)
        bx_copy(1, k).start()

    def st_r(k):
        bx_copy(1, k).wait_recv()
        bx_copy(2, k).wait_recv()
        total = slot_of(k, x)[...].astype(F32) + fin_a[:, cols(k)].astype(F32)
        sbuf[:, cols(k)] = (total + fin_b[:, cols(k)].astype(F32)).astype(BF16)
        for i in range(1, NY):
            by_copy(i, k).start()
        yr[rows(y * ROWS_J, ROWS_J), cols(k)] = sbuf[rows(y * ROWS_J, ROWS_J), cols(k)]

    def st_s(k):
        for i in range(1, NY):
            by_wait(i, k)
        part = yr[:, cols(k)]

        @pl.when(k < NH)
        def _():
            outf[k % 2] = nn(w1[...], part) + nn(w2[...], part)
            gacc[...] += nt(zbuf[:, cols(k + NH)], part)

        @pl.when(k >= NH)
        def _():
            outf[k % 2] = nn(dmat_t[...], part)

        cs[:, cols(k)] = outf[k % 2, oth_part, :].astype(BF16)
        be_copy(k).start()

    def st_t(k):
        be_copy(k).wait_recv()
        total = outf[k % 2, me_part, :] + cr[:, cols(k)].astype(F32)
        zs[:, cols(k)] = total.astype(BF16)
        for i in (1, 7, 2, 6, 3, 5, 4):
            bz_copy(i, k).start()
        zr[rows(z * TOK, TOK), cols(k)] = zs[rows(z * TOK, TOK), cols(k)]

    def st_v(k):
        for i in range(1, NZ):
            bz_wait(i, k)
        total = zr[0:TOK, cols(k)].astype(F32)
        for i in range(1, NZ):
            total += zr[i * TOK : (i + 1) * TOK, cols(k)].astype(F32)

        @pl.when(k < NH)
        def _():
            mixed_ref[:, cols(k)] = total.astype(BF16)

        @pl.when(k >= NH)
        def _():
            tgrad_ref[:, cols(k - NH)] = total.astype(BF16)

        for i in range(1, NY):
            by_copy(i, k).wait_send()
        be_copy(k).wait_send()
        for i in range(1, NZ):
            bz_copy(i, k).wait_send()

    def w_copies(k):
        s = k % 2
        return [
            pltpu.make_async_copy(stage.at[s, n], ref.at[:, cols(k)], wsem.at[n, s])
            for n, ref in enumerate((dwg_hbm, dwu_hbm, dwd_hbm))
        ]

    def st_weights(k):
        @pl.when(k == 0)
        def _():
            dgp_t[...] = dgp[...].astype(F32).T.astype(BF16)
            dup_t[...] = dup[...].astype(F32).T.astype(BF16)

        @pl.when(k >= 2)
        def _():
            for cp in w_copies(k - 2):
                cp.wait()

        part = xr[:, cols(k)]
        stage[k % 2, 0] = nn(dgp_t[...], part).astype(BF16)
        stage[k % 2, 1] = nn(dup_t[...], part).astype(BF16)
        stage[k % 2, 2] = nn(hid_t[...], xr[:, cols(k + NH)]).astype(BF16)
        for cp in w_copies(k):
            cp.start()

    def ge_copy():
        return remote(gsend, grecv, gess, gers, other)

    def gz_copy(i):
        src = gz_s.at[rows(((z + i) % NZ) * TOK, TOK)]
        return remote(src, gz_r.at[rows(z * TOK, TOK)], gzss.at[i - 1], gzrs.at[i - 1], at_z(i))

    def st_gate():
        lanes = iota((ROWS, 128), 1)
        j, _, _ = row_parts(iota((ROWS, 128), 0))
        hit = jnp.where(lanes == z * (NY * NC) + NC * j + c, 1.0, 0.0).astype(BF16)
        a, b, d = split3(gacc[...] * dmat_t[...].astype(F32))
        outf[0, :, 0:128] = nn(a, hit) + nn(b, hit) + nn(d, hit)
        gsend[...] = outf[0, oth_part, 0:128]
        ge_copy().start()
        ge_copy().wait_recv()
        gz_s[...] = outf[0, me_part, 0:128] + grecv[...]
        for i in range(1, NZ):
            gz_copy(i).start()
        gz_r[rows(z * TOK, TOK), :] = gz_s[rows(z * TOK, TOK), :]

    def st_gate_end():
        for i in range(1, NZ):
            dst = gz_r.at[rows(((z + NZ - i) % NZ) * TOK, TOK)]
            remote(dst, dst, gzss.at[i - 1], gzrs.at[i - 1], at_z(i)).wait_recv()
        total = gz_r[0:TOK, :]
        for i in range(1, NZ):
            total += gz_r[i * TOK : (i + 1) * TOK, :]
        own = meta[mine, :]
        lanes = iota((TOK, 128), 1).astype(F32)
        lane8 = iota((TOK, 8), 1)
        res = jnp.zeros((TOK, 8), F32)
        for k in range(8):
            val = jnp.sum(jnp.where(own[:, k : k + 1] == lanes, total, 0.0), axis=1, keepdims=True)
            res = jnp.where(lane8 == k, val, res)
        ggrad_ref[...] = res
        ge_copy().wait_send()
        for i in range(1, NZ):
            gz_copy(i).wait_send()

    def guarded(fn, k, low=0, high=N):
        @pl.when((k >= low) & (k < high))
        def _():
            fn(k)

    def step(i, carry):
        guarded(st_a, i, 2)
        guarded(st_b, i - 1)
        guarded(st_c, i - 2)
        guarded(st_d, i - 3)
        guarded(st_e, i - 4)
        guarded(st_f, i - 5)
        guarded(st_g, i - 7)
        k = i - 6 - NH
        guarded(st_w, k - SLOTS)
        guarded(st_p, k)
        guarded(st_q, k - 1)
        guarded(st_r, k - 2)
        guarded(st_s, k - 3)
        guarded(st_t, k - 4)
        guarded(st_v, k - 6)
        guarded(st_weights, k - NH - 1, 0, NH)
        return carry

    lax.fori_loop(0, N + NH + 6 + 7, step, 0)
    st_gate()
    for i in range(1, NZ):
        mz_copy(i).wait_send()
    me_copy.wait_send()
    for k in (NH - 2, NH - 1):
        for cp in w_copies(k):
            cp.wait()
    st_gate_end()


def body(tokens, cotangent, gate_prob, expert_ids, placement, gate_weight, up_weight, down_weight):
    toks, D = tokens.shape
    FQ = gate_weight.shape[1]
    N = 2 * D // CW
    R = NX * ROWS
    dma = pltpu.SemaphoreType.DMA
    vm = pltpu.VMEM
    vspec = pl.BlockSpec(memory_space=pltpu.VMEM)
    aspec = pl.BlockSpec(memory_space=pl.ANY)
    scratch = [
        vm((GROUP, 2 * D), BF16),
        vm((ROWS, 2 * D), BF16),
        vm((R, 2 * D), BF16),
        vm((FQ, D), BF16), vm((FQ, D), BF16), vm((FQ, D), BF16),
        vm((SLOTS, R, CW), BF16),
        vm((ROWS, 2 * D), BF16),
        vm((ROWS, 2 * D), BF16),
        vm((ROWS, 2 * D), BF16),
        vm((ROWS, 2 * D), BF16),
        vm((NZ * TOK, 2 * D), BF16),
        vm((NZ * TOK, 2 * D), BF16),
        vm((NZ * TOK, 2 * D), BF16),
        vm((NZ * TOK, 2 * D), BF16),
        vm((2, GROUP, CW), F32),
        vm((R, FQ), F32), vm((R, FQ), F32), vm((R, FQ), F32),
        vm((R, FQ), BF16), vm((R, FQ), BF16), vm((R, FQ), BF16),
        vm((FQ, R), BF16), vm((FQ, R), BF16), vm((FQ, R), BF16),
        vm((2, 3, FQ, CW), BF16),
        vm((GROUP, 128), F32),
        vm((ROWS, GROUP), BF16),
        vm((GROUP, ROWS), BF16),
        vm((GROUP, ROWS), BF16), vm((GROUP, ROWS), BF16),
        vm((ROWS, 128), F32),
        vm((GROUP, ROWS), F32),
        vm((NZ * TOK, 128), F32), vm((NZ * TOK, 128), F32),
        vm((NZ * TOK, 128), F32), vm((NZ * TOK, 128), F32),
        dma((5,)), dma(()),
        dma((NZ - 1, N)), dma((NZ - 1, N)), dma((N,)), dma((N,)),
        dma((NY - 1, N)), dma((NY - 1, N)), dma((3, N)), dma((3, N)),
        dma((3, N)), dma((3, N)), dma((NY - 1, N)), dma((NY - 1, N)),
        dma((N,)), dma((N,)), dma((NZ - 1, N)), dma((NZ - 1, N)),
        dma((NZ - 1,)), dma((NZ - 1,)), dma(()), dma(()),
        dma(()), dma(()), dma((NZ - 1,)), dma((NZ - 1,)), dma((3, 2)),
    ]
    mixed, token_grad, gate_grad, dwg, dwu, dwd = pl.pallas_call(
        kernel,
        out_shape=(
            jax.ShapeDtypeStruct((toks, D), BF16),
            jax.ShapeDtypeStruct((toks, D), BF16),
            jax.ShapeDtypeStruct(gate_prob.shape, F32),
            jax.ShapeDtypeStruct((FQ, D), BF16),
            jax.ShapeDtypeStruct((FQ, D), BF16),
            jax.ShapeDtypeStruct((FQ, D), BF16),
        ),
        in_specs=[aspec, aspec, vspec, vspec, vspec, aspec, aspec, aspec],
        out_specs=(vspec, vspec, vspec, aspec, aspec, aspec),
        scratch_shapes=scratch,
        compiler_params=pltpu.CompilerParams(
            collective_id=0, has_side_effects=True, vmem_limit_bytes=62 * 2**20
        ),
        cost_estimate=pl.CostEstimate(
            flops=9 * 2 * R * FQ * D, bytes_accessed=6 * FQ * D * 2, transcendentals=R * FQ
        ),
        name="moe_layer",
    )(
        tokens, cotangent, gate_prob, expert_ids, placement.reshape(1, -1),
        gate_weight[0], up_weight[0], down_weight[0],
    )
    return mixed, token_grad, gate_grad, dwg[None], dwu[None], dwd[None]


def solution(mesh):
    rows_spec = P(("dp", "expert"), None)
    weight_spec = P("expert", "dp", None)
    return jax.shard_map(
        body,
        mesh=mesh,
        in_specs=(rows_spec,) * 4 + (P(),) + (weight_spec,) * 3,
        out_specs=(rows_spec,) * 3 + (weight_spec,) * 3,
        check_vma=False,
    )
```

time: 443 us -> 278 us (0.63)
  Pallas kernels: 0 us -> 264 us
  waiting for transfers between devices: 207 us -> 0 us
  blocking collectives: 120 us -> 0 us
  matrix products: 45 us -> 0 us
  starting transfers between devices: 22.3 us -> 0 us
  local copies, waits for them, and re-layouts: 29.8 us -> 13.1 us
  between operations: 14 us -> 0.65 us
    pallas_call x0 -> x1, Pallas kernels: none -> 264 us  [body(): pl.pallas_call(kernel, out_shape=(jax.ShapeDtypeStruct((toks, D), BF16),...]
    all_to_all x2 -> x0, blocking collectives: 120 us -> none  [the longest x1 62.8 us: body(): lax.all_to_all(sent_rows, 'expert', split_axis=1, concat_axis=1, tiled=True)]
    reduce_scatter x2 -> x0, waiting for transfers between devices: 113 us -> none  [the longest x1 59.7 us: body(): lax.psum_scatter(out_part.astype(jnp.bfloat16), 'dp', scatter_dimension=0...]
    all_gather x2 -> x0, waiting for transfers between devices: 65.2 us -> none  [the longest x1 62.5 us: body(): lax.all_gather(got_grads, 'dp', axis=0, tiled=True)]
    dot_general x13 -> x0, matrix products: 45 us -> none  [the longest x1 6.06 us: body(): jnp.einsum('asjcd,jfd->asjcf', routed, up_weight, preferred_element_type=...]
    all_to_all x2 -> x0, waiting for transfers between devices: 28.2 us -> none  [the longest x1 28.2 us: body(): lax.all_to_all(summed[1].astype(jnp.bfloat16), 'expert', split_axis=1, co...]
    all_to_all x2 -> x0, starting transfers between devices: 21.7 us -> none  [the longest x1 10.9 us: body(): lax.all_to_all(summed[1].astype(jnp.bfloat16), 'expert', split_axis=1, co...]
    unnamed x29 -> x12, local copies, waits for them, and re-layouts: 1.08 us -> 13.1 us
  transfers between devices with their start and end apart: 6 -> 0, of which waited for: 5 -> 0; matrix products, arithmetic and copies ran while one was open for 12% -> 0% of each run, Pallas kernels for 0% -> 0%
where the time goes in v1:
time: 278 us; the launch traced here: 277 us
  Pallas kernels  264 us (95%)
  local copies, waits for them, and re-layouts  13.1 us (5%)
    pallas_call x1, Pallas kernels, body(): pl.pallas_call(kernel, out_shape=(jax.ShapeDtypeStruct((toks, D), BF16),...  264 us
    unnamed x12, local copies, waits for them, and re-layouts  13.1 us

profile of v1, /device:TPU:1, one launch (start us, length us, event | category | flops | bytes accessed | tf_op | source)
XLA Modules:
  0.0 277.4 jit_solution(6690551063934900197)
XLA Ops:
  0.6 1.4 copy.14.p_ref
  2.0 1.4 copy.15.ids_ref
  3.3 263.6 %moe_layer.1 = (bf16[16,4096]{1,0:T(8,128)(2,1)}, bf16[16,4096]{1,0:T(8,128)(2,1)}, f32[16,8]{1,0:T(8,128)}, bf16[192,4096]{1,0:T(8,128)(2,1)}, bf16[192,4096]{1,0:T(8,128)(2,1)}, /*index=5*/bf16[192,4096]{1,0:T(8,128)(2,1)}) custom-call(bf16[16,4096]{1,0:T(8,128)(2,1)} %x_hbm.1, bf16[16,4096]{1,0:T(8,128)(2,1)} %c_hbm.1, f32[16,8]{1,0:T(8,128)} %copy.14.p_ref, ...), custom_call_target="tpu_custom_call" | custom-call | flops 10871635968 | bytes 9437184 | tf_op jit(solution)/shard_map/moe_layer/pallas_call | solution.py:551
  266.9 1.4 copy.16
  268.3 1.6 copy.22
  269.9 1.6 copy.23
  271.4 0.0 copy-start.1
  271.4 2.8 %copy.24 = bf16[1,192,4096]{2,1,0:T(8,128)(2,1)} copy(bf16[1,192,4096]{2,1,0:T(8,128)(2,1)} %bitcast.9) | data formatting | bytes 3145728
  274.3 0.0 copy-done.1
  274.3 0.0 copy-start
  274.3 1.1 copy.25
  275.4 0.8 copy-done
  276.2 1.1 copy.26
Async XLA Ops:
  271.4 2.8 %copy-start.1 = (bf16[192,4096]{1,0:T(8,128)(2,1)S(1)}, bf16[192,4096]{1,0:T(8,128)(2,1)}, u32[]{:S(2)}) copy-start(bf16[192,4096]{1,0:T(8,128)(2,1)} %get-tuple-element.16) | copy-start | bytes 4718596
  274.3 2.0 copy-start

commit v2 on v1

v2 whole, which is shorter than its diff:
```python
import jax
import jax.numpy as jnp
from jax import lax
from jax.experimental import pallas as pl
from jax.experimental.pallas import tpu as pltpu
from jax.sharding import PartitionSpec as P

CAP = 3
NX, NZ, NY, NC = 4, 8, 4, 2
MESH = pl.DeviceIdType.MESH
F32, BF16 = jnp.float32, jnp.bfloat16

TOK = 16
BLOCKS = NC * NZ
GROUP = BLOCKS * TOK
ROWS_J = BLOCKS * CAP
ROWS = NY * ROWS_J
CW = 512
PSLOTS = 4
SLOTS = 4
WIDE_OUT = (6, 7, 9, 11, 13, 14)
WIDE_BACK = (9, 12)


def nt(a, b):
    return lax.dot_general(a, b, (((1,), (1,)), ((), ())), preferred_element_type=F32)


def nn(a, b):
    return jnp.dot(a, b, preferred_element_type=F32)


def split3(v):
    a = v.astype(BF16)
    rest = v - a.astype(F32)
    b = rest.astype(BF16)
    return a, b, (rest - b.astype(F32)).astype(BF16)


def iota(shape, dim):
    return lax.broadcasted_iota(jnp.int32, shape, dim)


def row_parts(r):
    q = r >> 4
    j = (q >= 3).astype(jnp.int32) + (q >= 6).astype(jnp.int32) + (q >= 9).astype(jnp.int32)
    return j, q - 3 * j, r & 15


def kernel(
    x_hbm, c_hbm, own_ref, wg_hbm, wu_hbm, wd_hbm,
    mixed_ref, tgrad_ref, ggrad_ref, dwg_hbm, dwu_hbm, dwd_hbm,
    zbuf, zc, sbuf, sc, xr, wg, wu, wd, pb, rly, fin_a, fin_b, ybuf, yr, cs, cr, zs, zr,
    csc, zsc, xsc, xrc,
    g_acc, u_acc, d_acc, hid, dgp, dup, hid_t, dgp_t, dup_t, stage,
    meta, dmat, dmat_t, w1, w2, prow, gacc, gtmp, gsend, grecv, gz_s, gz_r,
    load_sem,
    zss, zrs, ess, ers, yss, yrs, xss, xrs,
    bxss, bxrs, byss, byrs, bess, bers, bzss, bzrs, wxss, wxrs, vxss, vxrs,
    mzss, mzrs, mess, mers, mxss, mxrs, gess, gers, gzss, gzrs, wsem,
):
    D = x_hbm.shape[1]
    NH = D // CW
    N = 2 * NH
    x = lax.axis_index("dp")
    e = lax.axis_index("expert")
    z, y, c = e // (NY * NC), (e // NC) % NY, e % NC
    right, left, opp = (x + 1) % NX, (x + 3) % NX, (x + 2) % NX

    def at_z(i):
        return {"expert": (((z + i) % NZ) * NY + y) * NC + c}

    def at_y(i):
        return {"expert": (z * NY + (y + i) % NY) * NC + c}

    def at_x(i):
        return {"dp": (x + i) % NX}

    other = {"expert": (z * NY + y) * NC + (1 - c)}

    def cols(k):
        return pl.ds(pl.multiple_of(k * CW, CW), CW)

    def rows(start, size):
        return pl.ds(pl.multiple_of(start, 16), size)

    def among(k, chosen):
        hit = k == chosen[0]
        for v in chosen[1:]:
            hit = hit | (k == v)
        return hit

    def place_in(k, chosen):
        return sum((k > v).astype(jnp.int32) for v in chosen)

    def either(k, chosen, wide, narrow):
        hit = among(k, chosen)

        @pl.when(hit)
        def _():
            wide(k)

        @pl.when(jnp.logical_not(hit))
        def _():
            narrow(k)

    def remote(src, dst, ss, rs, dev):
        return pltpu.make_async_remote_copy(
            src_ref=src, dst_ref=dst, send_sem=ss, recv_sem=rs, device_id=dev, device_id_type=MESH
        )

    def arrived(dst, ss, rs, dev):
        remote(dst, dst, ss, rs, dev).wait_recv()

    def all_sent(ref, sem):
        remote(ref, ref, sem, sem, {"dp": right}).wait_send()

    def all_arrived(ref, sem):
        remote(ref, ref, sem, sem, {"dp": right}).wait_recv()

    z_order = (1, 7, 2, 6, 3, 5, 4)
    seven, three = pl.ds(0, (NZ - 1) * TOK), pl.ds(0, (NY - 1) * ROWS_J)
    mine = rows((c * NZ + z) * TOK, TOK)
    me_part = rows(c * NZ * TOK, NZ * TOK)
    oth_part = rows((1 - c) * NZ * TOK, NZ * TOK)

    def z_part(i):
        return rows((c * NZ + (z + NZ - i) % NZ) * TOK, TOK)

    def y_part(i):
        return rows(((y + NY - i) % NY) * ROWS_J, ROWS_J)

    y_own = rows(y * ROWS_J, ROWS_J)

    def y_to(i):
        return rows(((y + i) % NY) * ROWS_J, ROWS_J)

    loads = [
        pltpu.make_async_copy(x_hbm, zbuf.at[mine, pl.ds(0, D)], load_sem.at[0]),
        pltpu.make_async_copy(c_hbm, zbuf.at[mine, pl.ds(D, D)], load_sem.at[1]),
        pltpu.make_async_copy(wg_hbm, wg, load_sem.at[2]),
        pltpu.make_async_copy(wu_hbm, wu, load_sem.at[3]),
        pltpu.make_async_copy(wd_hbm, wd, load_sem.at[4]),
    ]
    for cp in loads:
        cp.start()
    barrier = pltpu.get_barrier_semaphore()
    peers = [at_z(i) for i in range(1, NZ)] + [at_y(i) for i in range(1, NY)]
    peers += [at_x(i) for i in range(1, NX)] + [other]
    for dev in peers:
        pl.semaphore_signal(barrier, inc=1, device_id=dev, device_id_type=MESH)
    meta[x, mine, :] = own_ref[...]
    loads[0].wait()
    loads[1].wait()
    pl.semaphore_wait(barrier, len(peers))

    def z_copy(i, k):
        part = (mine, cols(k))
        return remote(zbuf.at[part], zbuf.at[part], zss.at[0, k], zrs.at[0, k], at_z(i))

    def e_copy(k):
        part = (me_part, cols(k))
        return remote(zbuf.at[part], zbuf.at[part], ess.at[k], ers.at[k], other)

    def y_copy(i, k):
        dst = xr.at[x, y_own, cols(k)]
        return remote(sbuf.at[k % SLOTS, y_to(i)], dst, yss.at[k], yrs.at[k], at_y(i))

    def half(k, h):
        return pl.ds(pl.multiple_of(k * CW + h * (CW // 2), CW // 2), CW // 2)

    def x_copy(d, k):
        if d < 2:
            ref = xr.at[x, :, cols(k)]
        else:
            ref = xr.at[right if d == 3 else left, :, half(k, d - 2)]
        dev = {"dp": left if d % 2 else right}
        return remote(ref, ref, xss.at[k], xrs.at[d, k], dev)

    def x_wait(d, k):
        if d < 2:
            ref = xr.at[right if d else left, :, cols(k)]
        else:
            ref = xr.at[opp, :, half(k, d - 2)]
        arrived(ref, xss.at[k], xrs.at[d, k], {"dp": right})

    def wx_copy(i, k):
        w = place_in(k, WIDE_OUT)
        dst = zc.at[w, x, mine]
        return remote(zbuf.at[mine, cols(k)], dst, wxss.at[i - 1, w], wxrs.at[i - 1, w], at_x(i))

    def wz_copy(d, s, k):
        ref = zc.at[place_in(k, WIDE_OUT), :, z_part(NZ - s if d else s)]
        return remote(ref, ref, zss.at[0, k], zrs.at[2 * s + d, k], at_z(NZ - 1 if d else 1))

    def wz_wait(d, s, k):
        ref = zc.at[place_in(k, WIDE_OUT), :, z_part(NZ - s - 1 if d else s + 1)]
        arrived(ref, zss.at[0, k], zrs.at[2 * s + d, k], at_z(1))

    z_ring = [(d, s) for s in range(4) for d in range(2)][:7]

    def we_copy(k):
        ref = zc.at[place_in(k, WIDE_OUT), :, me_part]
        return remote(ref, ref, ess.at[k], ers.at[k], other)

    def wy_copy(i, k):
        src = sc.at[place_in(k, WIDE_OUT) % 2, :, y_to(i)]
        dst = xr.at[:, y_own, cols(k)]
        return remote(src, dst, yss.at[k], yrs.at[k], at_y(i))

    def bx_copy(d, h, k):
        rdev, ddev = (right, left) if h else (left, right)
        part = pl.ds(h * (CW // 2), CW // 2)
        if d == 0:
            src, dst, dev = opp, rly, rdev
        elif d == 1:
            src, dst, dev = rdev, fin_b, rdev
        else:
            src, dst, dev = ddev, fin_a, ddev
        n = 2 * d + h
        return remote(
            pb.at[k % PSLOTS, src, :, part], dst.at[:, half(k, h)], bxss.at[k], bxrs.at[n, k], {"dp": dev}
        )

    def by_copy(i, k):
        dst = yr.at[y_own, cols(k)]
        return remote(ybuf.at[k % SLOTS, y_to(i)], dst, byss.at[k], byrs.at[k], at_y(i))

    def be_copy(k):
        return remote(cs.at[k % SLOTS], cr.at[:, cols(k)], bess.at[k], bers.at[k], other)

    def bz_copy(i, k):
        src = zs.at[k % SLOTS, rows(((z + i) % NZ) * TOK, TOK)]
        dst = zr.at[rows(z * TOK, TOK), cols(k)]
        return remote(src, dst, bzss.at[k], bzrs.at[k], at_z(i))

    W = len(WIDE_BACK)

    def v_y(k):
        return place_in(k, WIDE_BACK)

    def v_e(k, part):
        return zc.at[W + place_in(k, WIDE_BACK), :, part]

    def vy_copy(i, k):
        dst = zc.at[v_y(k), :, y_own]
        return remote(pb.at[k % PSLOTS, :, y_to(i)], dst, byss.at[k], byrs.at[k], at_y(i))

    def ve_copy(k):
        w = v_y(k)
        return remote(csc.at[w], v_e(k, pl.ds(0, NZ * TOK)), bess.at[k], bers.at[k], other)

    def vz_copy(i, k):
        src = zsc.at[v_y(k), :, rows(((z + i) % NZ) * TOK, TOK)]
        dst = v_e(k, rows(NZ * TOK + z * TOK, TOK))
        return remote(src, dst, bzss.at[k], bzrs.at[k], at_z(i))

    def vx_copy(i, k):
        w = v_y(k)
        return remote(
            xsc.at[w, (x + i) % NX], xrc.at[w, x], vxss.at[i - 1, w], vxrs.at[i - 1, w], at_x(i)
        )

    def mz_copy(i):
        ref = meta.at[x, mine]
        return remote(ref, ref, mzss.at[i - 1], mzrs.at[i - 1], at_z(i))

    me_copy = remote(meta.at[x, me_part], meta.at[x, me_part], mess, mers, other)

    def mx_copy(i):
        return remote(meta.at[x], meta.at[x], mxss.at[i - 1], mxrs.at[i - 1], at_x(i))

    def route(g, own):
        info = meta[g]
        lane = iota((GROUP, 128), 1)
        target = jnp.where(lane < NY, z * (NY * NC) + c + NC * lane, -1).astype(F32)
        used = jnp.zeros((GROUP, 128), F32)
        prob = jnp.zeros((GROUP, 128), F32)
        for k in range(8):
            hit = info[:, k : k + 1] == target
            used += jnp.where(hit, 1.0, 0.0)
            prob += jnp.where(hit, info[:, 8 + k : 9 + k], 0.0)
        t_row, t_col = iota((GROUP, GROUP), 0), iota((GROUP, GROUP), 1)
        before = ((t_row >> 4) == (t_col >> 4)) & (t_col < t_row)
        used_b = used.astype(BF16)
        rank_b = nn(jnp.where(before, 1.0, 0.0).astype(BF16), used_b).astype(BF16)
        probs3 = split3(prob)
        rj, _, _ = row_parts(iota((ROWS, 128), 0))
        spread = jnp.where(rj == iota((ROWS, 128), 1), 1.0, 0.0).astype(BF16)
        rj, rrank, rblk = row_parts(iota((ROWS, GROUP), 0))
        keep = rblk == (iota((ROWS, GROUP), 1) >> 4)
        keep = keep & (nt(spread, rank_b) == rrank.astype(F32))
        d_f = jnp.where(keep, nt(spread, used_b), 0.0)
        dmat[g] = d_f.astype(BF16)
        weight = nt(spread, probs3[0]) + nt(spread, probs3[1]) + nt(spread, probs3[2])
        prow[g] = jnp.broadcast_to(jnp.sum(d_f * weight, axis=1, keepdims=True), (ROWS, 128))
        rj, _, _ = row_parts(iota((128, ROWS), 1))
        spread_t = jnp.where(rj == iota((128, ROWS), 0), 1.0, 0.0).astype(BF16)
        rj, rrank, rblk = row_parts(iota((GROUP, ROWS), 1))
        keep = rblk == (iota((GROUP, ROWS), 0) >> 4)
        keep = keep & (nn(rank_b, spread_t) == rrank.astype(F32))
        d_t = jnp.where(keep, nn(used_b, spread_t), 0.0)
        dmat_t[g] = d_t.astype(BF16)
        if own:
            weight = nn(probs3[0], spread_t) + nn(probs3[1], spread_t) + nn(probs3[2], spread_t)
            weight = d_t * weight
            w1[...] = weight.astype(BF16)
            w2[...] = (weight - weight.astype(BF16).astype(F32)).astype(BF16)

    def route_other(i):
        @pl.when(i == 0)
        def _():
            for j in range(1, NX):
                arrived(meta.at[(x + NX - j) % NX], mxss.at[j - 1], mxrs.at[j - 1], at_x(j))

        route((x + 1 + i) % NX, False)

    def st_x(k):
        @pl.when(among(k, WIDE_OUT))
        def _():
            for i in (2, 1, 3):
                wx_copy(i, k).start()
            zc[place_in(k, WIDE_OUT), x, mine, :] = zbuf[mine, cols(k)]

    def st_a():
        def wide(k):
            w = place_in(k, WIDE_OUT)
            for i in range(1, NX):
                arrived(zc.at[w, (x + NX - i) % NX, mine], wxss.at[i - 1, w], wxrs.at[i - 1, w], at_x(i))
            wz_copy(0, 0, k).start()
            wz_copy(1, 0, k).start()

        def narrow(k):
            for i in z_order:
                z_copy(i, k).start()

        return wide, narrow

    wide_a, narrow_a = st_a()

    def st_az(k):
        @pl.when(among(k, WIDE_OUT))
        def _():
            wide_a(k)

    def st_an(k):
        @pl.when(jnp.logical_not(among(k, WIDE_OUT)))
        def _():
            narrow_a(k)

    def st_ring(s):
        def run(k):
            @pl.when(among(k, WIDE_OUT))
            def _():
                for d in range(2):
                    wz_wait(d, s - 1, k)
                    if (d, s) in z_ring:
                        wz_copy(d, s, k).start()

        return run

    def st_b(k):
        def wide(k):
            wz_wait(0, 3, k)
            we_copy(k).start()

        def narrow(k):
            all_arrived(zbuf.at[seven, cols(k)], zrs.at[0, k])
            e_copy(k).start()

        either(k, WIDE_OUT, wide, narrow)

    def st_c(k):
        def wide(k):
            w = place_in(k, WIDE_OUT)
            arrived(zc.at[w, :, oth_part], ess.at[k], ers.at[k], other)

            def one(g, carry):
                scale = jnp.where(k < NH, 1.0, prow[g, :, 0:1])
                sc[w % 2, g] = (nn(dmat[g], zc[w, g]) * scale).astype(BF16)
                return carry

            lax.fori_loop(0, NX, one, 0)
            for i in range(1, NY):
                wy_copy(i, k).start()
            xr[:, y_own, cols(k)] = sc[w % 2, :, y_own, :]

        def narrow(k):
            arrived(zbuf.at[oth_part, cols(k)], ess.at[k], ers.at[k], other)
            scale = jnp.where(k < NH, 1.0, prow[x, :, 0:1])
            sbuf[k % SLOTS] = (nn(dmat[x], zbuf[:, cols(k)]) * scale).astype(BF16)
            for i in range(1, NY):
                y_copy(i, k).start()
            xr[x, y_own, cols(k)] = sbuf[k % SLOTS, y_own, :]

        either(k, WIDE_OUT, wide, narrow)

    def st_d(k):
        @pl.when(jnp.logical_not(among(k, WIDE_OUT)))
        def _():
            all_arrived(xr.at[x, three, cols(k)], yrs.at[k])
            x_copy(0, k).start()
            x_copy(1, k).start()

    def st_e(k):
        @pl.when(jnp.logical_not(among(k, WIDE_OUT)))
        def _():
            x_wait(0, k)
            x_copy(2, k).start()
            x_wait(1, k)
            x_copy(3, k).start()

    def all_rows(k):
        return xr[:, :, cols(k)].reshape(NX * ROWS, CW)

    def st_f(k):
        def wide(k):
            all_arrived(xr.at[:, three, cols(k)], yrs.at[k])

        def narrow(k):
            x_wait(2, k)
            x_wait(3, k)

        either(k, WIDE_OUT, wide, narrow)

        @pl.when(k < NH)
        def _():
            part = all_rows(k)
            g_acc[...] += nt(part, wg[:, cols(k)])
            u_acc[...] += nt(part, wu[:, cols(k)])

        @pl.when(k >= NH)
        def _():
            d_acc[...] += nt(all_rows(k), wd[:, cols(k - NH)])

        @pl.when(k == NH - 1)
        def _():
            def one(i, carry):
                part = rows(i * 64, 64)
                g, u = g_acc[part, :], u_acc[part, :]
                sig = 1.0 / (1.0 + jnp.exp(-g))
                silu = g * sig
                hid[part, :] = (silu * u).astype(BF16)
                g_acc[part, :] = u * (sig * (1.0 + g * (1.0 - sig)))
                u_acc[part, :] = silu
                return carry

            lax.fori_loop(0, NX * ROWS // 64, one, 0)

        @pl.when(k == N - 1)
        def _():
            def one(i, carry):
                part = rows(i * 64, 64)
                dh = d_acc[part, :]
                dgp[part, :] = (dh * g_acc[part, :]).astype(BF16)
                dup[part, :] = (dh * u_acc[part, :]).astype(BF16)
                return carry

            lax.fori_loop(0, NX * ROWS // 64, one, 0)

    def st_gy(k):
        def wide(k):
            all_sent(sc.at[0, :, three], yss.at[k])

        def narrow(k):
            all_sent(sbuf.at[0, three], yss.at[k])

        either(k, WIDE_OUT, wide, narrow)

    def st_g(k):
        def wide(k):
            for i in range(1, NX):
                wx_copy(i, k).wait_send()
            all_sent(zc.at[0, :, seven], zss.at[0, k])
            we_copy(k).wait_send()

        def narrow(k):
            all_sent(zbuf.at[seven, cols(k)], zss.at[0, k])
            e_copy(k).wait_send()
            all_sent(xr.at[0:3, :, cols(k)], xss.at[k])

        either(k, WIDE_OUT, wide, narrow)

    def st_w(k):
        def wide(k):
            all_sent(sc.at[0, :, three], byss.at[k])

        def narrow(k):
            all_sent(pb.at[0, 0:3], bxss.at[k])

        either(k, WIDE_BACK, wide, narrow)

    def st_p(k):
        def store(v):
            pb[k % PSLOTS] = v.astype(BF16).reshape(NX, ROWS, CW)

        @pl.when(k < NH)
        def _():
            store(nn(hid[...], wd[:, cols(k)]))

        @pl.when(k >= NH)
        def _():
            part = cols(k - NH)
            store(nn(dgp[...], wg[:, part]) + nn(dup[...], wu[:, part]))

        def wide(k):
            for i in range(1, NY):
                vy_copy(i, k).start()
            zc[v_y(k), :, y_own, :] = pb[k % PSLOTS, :, y_own, :]

        def narrow(k):
            for d in (0, 2):
                for h in range(2):
                    bx_copy(d, h, k).start()

        either(k, WIDE_BACK, wide, narrow)

    def st_q(k):
        @pl.when(jnp.logical_not(among(k, WIDE_BACK)))
        def _():
            for h in range(2):
                bx_copy(0, h, k).wait_recv()
                part = pl.ds(h * (CW // 2), CW // 2)
                ref = pb.at[k % PSLOTS, right if h else left, :, part]
                ref[...] = (rly[:, half(k, h)].astype(F32) + ref[...].astype(F32)).astype(BF16)
                bx_copy(1, h, k).start()

    def st_r(k):
        @pl.when(jnp.logical_not(among(k, WIDE_BACK)))
        def _():
            for h in range(2):
                bx_copy(1, h, k).wait_recv()
                bx_copy(2, h, k).wait_recv()
            total = pb[k % PSLOTS, x].astype(F32) + fin_a[:, cols(k)].astype(F32)
            ybuf[k % SLOTS] = (total + fin_b[:, cols(k)].astype(F32)).astype(BF16)
            for i in range(1, NY):
                by_copy(i, k).start()
            yr[y_own, cols(k)] = ybuf[k % SLOTS, y_own, :]

    def st_s(k):
        def wide(k):
            w = v_y(k)
            all_arrived(zc.at[w, :, three], byrs.at[k])

            def one(g, carry):
                csc[w, g] = nn(dmat_t[g, oth_part, :], zc[w, g, 0:ROWS, :]).astype(BF16)
                return carry

            lax.fori_loop(0, NX, one, 0)
            ve_copy(k).start()

        def narrow(k):
            all_arrived(yr.at[three, cols(k)], byrs.at[k])
            part = yr[:, cols(k)]

            @pl.when(k < NH)
            def _():
                v = nn(w1[oth_part, :], part) + nn(w2[oth_part, :], part)
                cs[k % SLOTS] = v.astype(BF16)

                def wide_c(k):
                    gacc[...] += nt(zc[place_in(k, WIDE_OUT), x], part)

                def narrow_c(k):
                    gacc[...] += nt(zbuf[:, cols(k)], part)

                either(k + NH, WIDE_OUT, wide_c, narrow_c)

            @pl.when(k >= NH)
            def _():
                cs[k % SLOTS] = nn(dmat_t[x, oth_part, :], part).astype(BF16)

            be_copy(k).start()

        either(k, WIDE_BACK, wide, narrow)

    def st_t(k):
        def wide(k):
            w = v_y(k)
            arrived(v_e(k, pl.ds(0, NZ * TOK)), bess.at[k], bers.at[k], other)

            def one(g, carry):
                v = nn(dmat_t[g, me_part, :], zc[w, g, 0:ROWS, :])
                zsc[w, g] = (v + zc[W + w, g, 0 : NZ * TOK, :].astype(F32)).astype(BF16)
                return carry

            lax.fori_loop(0, NX, one, 0)
            for i in z_order:
                vz_copy(i, k).start()
            here = rows(NZ * TOK + z * TOK, TOK)
            zc[W + w, :, here, :] = zsc[w, :, rows(z * TOK, TOK), :]

        def narrow(k):
            be_copy(k).wait_recv()
            part = yr[:, cols(k)]

            @pl.when(k < NH)
            def _():
                v = nn(w1[me_part, :], part) + nn(w2[me_part, :], part)
                zs[k % SLOTS] = (v + cr[:, cols(k)].astype(F32)).astype(BF16)

            @pl.when(k >= NH)
            def _():
                v = nn(dmat_t[x, me_part, :], part)
                zs[k % SLOTS] = (v + cr[:, cols(k)].astype(F32)).astype(BF16)

            for i in z_order:
                bz_copy(i, k).start()
            zr[rows(z * TOK, TOK), cols(k)] = zs[k % SLOTS, rows(z * TOK, TOK), :]

        either(k, WIDE_BACK, wide, narrow)

    def z_back(i):
        return ((z + NZ - i) % NZ) * TOK

    def st_v(k):
        def wide(k):
            w = v_y(k)
            all_arrived(v_e(k, pl.ds(NZ * TOK, (NZ - 1) * TOK)), bzrs.at[k])
            total = zc[W + w, :, NZ * TOK : (NZ + 1) * TOK, :].astype(F32)
            for i in range(1, NZ):
                total += zc[W + w, :, (NZ + i) * TOK : (NZ + i + 1) * TOK, :].astype(F32)
            xsc[w] = total.astype(BF16)
            for i in (2, 1, 3):
                vx_copy(i, k).start()
            xrc[w, x] = xsc[w, x]

        def narrow(k):
            all_arrived(zr.at[seven, cols(k)], bzrs.at[k])
            total = zr[0:TOK, cols(k)].astype(F32)
            for i in range(1, NZ):
                total += zr[i * TOK : (i + 1) * TOK, cols(k)].astype(F32)

            @pl.when(k < NH)
            def _():
                mixed_ref[:, cols(k)] = total.astype(BF16)

            @pl.when(k >= NH)
            def _():
                tgrad_ref[:, cols(k - NH)] = total.astype(BF16)

        either(k, WIDE_BACK, wide, narrow)

    def st_u(k):
        @pl.when(among(k, WIDE_BACK))
        def _():
            w = v_y(k)
            for i in range(1, NX):
                part = xrc.at[w, (x + NX - i) % NX]
                arrived(part, vxss.at[i - 1, w], vxrs.at[i - 1, w], at_x(i))
            total = xrc[w, 0].astype(F32)
            for i in range(1, NX):
                total += xrc[w, i].astype(F32)
            tgrad_ref[:, cols(k - NH)] = total.astype(BF16)
            for i in range(1, NX):
                vx_copy(i, k).wait_send()

    def st_hy(k):
        @pl.when(jnp.logical_not(among(k, WIDE_BACK)))
        def _():
            all_sent(ybuf.at[0, three], byss.at[k])

    def st_he(k):
        either(k, WIDE_BACK, lambda k: ve_copy(k).wait_send(), lambda k: be_copy(k).wait_send())

    def st_hz(k):
        def wide(k):
            all_sent(zc.at[0, :, seven], bzss.at[k])

        def narrow(k):
            all_sent(zs.at[0, seven], bzss.at[k])

        either(k, WIDE_BACK, wide, narrow)

    def w_copies(k):
        return [
            pltpu.make_async_copy(stage.at[n], ref.at[:, cols(k)], wsem.at[n])
            for n, ref in enumerate((dwg_hbm, dwu_hbm, dwd_hbm))
        ]

    def st_weights(k):
        @pl.when(k == 0)
        def _():
            hid_t[...] = hid[...].astype(F32).T.astype(BF16)
            dgp_t[...] = dgp[...].astype(F32).T.astype(BF16)
            dup_t[...] = dup[...].astype(F32).T.astype(BF16)

        @pl.when(k >= 1)
        def _():
            for cp in w_copies(k - 1):
                cp.wait()

        part = all_rows(k)
        stage[0] = nn(dgp_t[...], part).astype(BF16)
        stage[1] = nn(dup_t[...], part).astype(BF16)
        stage[2] = nn(hid_t[...], all_rows(k + NH)).astype(BF16)
        for cp in w_copies(k):
            cp.start()

    def ge_copy():
        return remote(gsend, grecv, gess, gers, other)

    def gz_copy(i):
        src = gz_s.at[rows(((z + i) % NZ) * TOK, TOK)]
        return remote(src, gz_r.at[rows(z * TOK, TOK)], gzss.at[i - 1], gzrs.at[i - 1], at_z(i))

    def st_gate(k):
        lanes = iota((ROWS, 128), 1)
        j, _, _ = row_parts(iota((ROWS, 128), 0))
        hit = jnp.where(lanes == z * (NY * NC) + NC * j + c, 1.0, 0.0).astype(BF16)
        a, b, d = split3(gacc[...] * dmat_t[x].astype(F32))
        gtmp[...] = nn(a, hit) + nn(b, hit) + nn(d, hit)
        gsend[...] = gtmp[oth_part, :]
        ge_copy().start()

    def st_gate_z(k):
        ge_copy().wait_recv()
        gz_s[...] = gtmp[me_part, :] + grecv[...]
        for i in z_order:
            gz_copy(i).start()
        gz_r[rows(z * TOK, TOK), :] = gz_s[rows(z * TOK, TOK), :]

    def st_gate_end(k):
        for i in range(1, NZ):
            arrived(gz_r.at[rows(z_back(i), TOK)], gzss.at[i - 1], gzrs.at[i - 1], at_z(i))
        total = gz_r[0:TOK, :]
        for i in range(1, NZ):
            total += gz_r[i * TOK : (i + 1) * TOK, :]
        own = own_ref[...]
        lanes = iota((TOK, 128), 1).astype(F32)
        lane8 = iota((TOK, 8), 1)
        res = jnp.zeros((TOK, 8), F32)
        for k in range(8):
            val = jnp.sum(jnp.where(own[:, k : k + 1] == lanes, total, 0.0), axis=1, keepdims=True)
            res = jnp.where(lane8 == k, val, res)
        ggrad_ref[...] = res
        ge_copy().wait_send()
        for i in range(1, NZ):
            gz_copy(i).wait_send()

    def guarded(fn, k, low=0, high=N):
        @pl.when((k >= low) & (k < high))
        def _():
            fn(k)

    START = 3
    for i in z_order:
        mz_copy(i).start()
    for k in range(2):
        for i in z_order:
            z_copy(i, k).start()
    for i in range(1, NZ):
        arrived(meta.at[x, z_part(i)], mzss.at[i - 1], mzrs.at[i - 1], at_z(i))
    me_copy.start()
    g_acc[...] = jnp.zeros_like(g_acc)
    u_acc[...] = jnp.zeros_like(u_acc)
    d_acc[...] = jnp.zeros_like(d_acc)
    gacc[...] = jnp.zeros_like(gacc)
    arrived(meta.at[x, oth_part], mess, mers, other)
    for i in (2, 1, 3):
        mx_copy(i).start()
    route(x, True)
    loads[2].wait()
    loads[3].wait()
    loads[4].wait()

    def step(i, carry):
        guarded(st_x, i + 3)
        guarded(st_az, i + 2)
        guarded(st_ring(1), i + 1)
        guarded(st_ring(2), i)
        guarded(st_ring(3), i - 1)
        guarded(st_an, i - 1)
        guarded(st_gy, i - 7)
        guarded(st_d, i - 5)
        guarded(st_c, i - 4)
        guarded(st_b, i - 3)
        guarded(st_e, i - 6)
        guarded(route_other, i - 4, 0, NX - 1)
        guarded(st_f, i - 7)
        guarded(st_g, i - 10)
        k = i - 6 - NH
        guarded(st_w, k - PSLOTS)
        guarded(st_p, k)
        guarded(st_q, k - 1)
        guarded(st_hy, k - 5)
        guarded(st_r, k - 2)
        guarded(st_s, k - 4)
        guarded(st_t, k - 5)
        guarded(st_gate, k - 4 - NH, 0, 1)
        guarded(st_gate_z, k - 5 - NH, 0, 1)
        guarded(st_gate_end, k - 7 - NH, 0, 1)
        guarded(st_v, k - 7)
        guarded(st_he, k - 7)
        guarded(st_hz, k - 8)
        guarded(st_u, k - 9)
        guarded(st_weights, k - NH - 1, 0, NH)
        return carry

    lax.fori_loop(START, N + NH + 6 + 9, step, 0)
    for i in range(1, NZ):
        mz_copy(i).wait_send()
    me_copy.wait_send()
    for i in range(1, NX):
        mx_copy(i).wait_send()
    for cp in w_copies(NH - 1):
        cp.wait()


def settle(*refs):
    for i in range(len(refs) // 2):
        refs[len(refs) // 2 + i][...] = refs[i][...]


def body(tokens, cotangent, gate_prob, expert_ids, placement, gate_weight, up_weight, down_weight):
    toks, D = tokens.shape
    FQ = gate_weight.shape[1]
    N = 2 * D // CW
    R = NX * ROWS
    NT = NZ * TOK
    WO, WB = len(WIDE_OUT), len(WIDE_BACK)
    match = expert_ids[:, :, None] == jnp.arange(placement.shape[0], dtype=jnp.int32)
    slots = jnp.sum(jnp.where(match, placement, 0), axis=2).astype(F32)
    own = jnp.concatenate([slots, gate_prob, jnp.zeros((toks, 112), F32)], axis=1)
    dma = pltpu.SemaphoreType.DMA
    vm = pltpu.VMEM
    vspec = pl.BlockSpec(memory_space=pltpu.VMEM)
    aspec = pl.BlockSpec(memory_space=pl.ANY)
    scratch = [
        vm((GROUP, 2 * D), BF16),
        vm((WO, NX, GROUP, CW), BF16),
        vm((SLOTS, ROWS, CW), BF16),
        vm((2, NX, ROWS, CW), BF16),
        vm((NX, ROWS, 2 * D), BF16),
        vm((FQ, D), BF16), vm((FQ, D), BF16), vm((FQ, D), BF16),
        vm((PSLOTS, NX, ROWS, CW), BF16),
        vm((ROWS, 2 * D), BF16),
        vm((ROWS, 2 * D), BF16),
        vm((ROWS, 2 * D), BF16),
        vm((SLOTS, ROWS, CW), BF16),
        vm((ROWS, 2 * D), BF16),
        vm((SLOTS, NT, CW), BF16),
        vm((NT, 2 * D), BF16),
        vm((SLOTS, NT, CW), BF16),
        vm((NT, 2 * D), BF16),
        vm((WB, NX, NT, CW), BF16),
        vm((WB, NX, NT, CW), BF16),
        vm((WB, NX, TOK, CW), BF16),
        vm((WB, NX, TOK, CW), BF16),
        vm((R, FQ), F32), vm((R, FQ), F32), vm((R, FQ), F32),
        vm((R, FQ), BF16), vm((R, FQ), BF16), vm((R, FQ), BF16),
        vm((FQ, R), BF16), vm((FQ, R), BF16), vm((FQ, R), BF16),
        vm((3, FQ, CW), BF16),
        vm((NX, GROUP, 128), F32),
        vm((NX, ROWS, GROUP), BF16),
        vm((NX, GROUP, ROWS), BF16),
        vm((GROUP, ROWS), BF16), vm((GROUP, ROWS), BF16),
        vm((NX, ROWS, 128), F32),
        vm((GROUP, ROWS), F32),
        vm((GROUP, 128), F32),
        vm((NT, 128), F32), vm((NT, 128), F32),
        vm((NT, 128), F32), vm((NT, 128), F32),
        dma((5,)),
        dma((1, N)), dma((NZ - 1, N)), dma((N,)), dma((N,)),
        dma((N,)), dma((N,)), dma((N,)), dma((4, N)),
        dma((N,)), dma((6, N)), dma((N,)), dma((N,)),
        dma((N,)), dma((N,)), dma((N,)), dma((N,)),
        dma((NX - 1, WO)), dma((NX - 1, WO)), dma((NX - 1, WB)), dma((NX - 1, WB)),
        dma((NZ - 1,)), dma((NZ - 1,)), dma(()), dma(()), dma((NX - 1,)), dma((NX - 1,)),
        dma(()), dma(()), dma((NZ - 1,)), dma((NZ - 1,)), dma((3,)),
    ]
    shapes = (
        jax.ShapeDtypeStruct((toks, D), BF16),
        jax.ShapeDtypeStruct((toks, D), BF16),
        jax.ShapeDtypeStruct(gate_prob.shape, F32),
        jax.ShapeDtypeStruct((FQ, D), BF16),
        jax.ShapeDtypeStruct((FQ, D), BF16),
        jax.ShapeDtypeStruct((FQ, D), BF16),
    )
    outs = pl.pallas_call(
        kernel,
        out_shape=shapes,
        in_specs=[aspec, aspec, vspec, aspec, aspec, aspec],
        out_specs=(vspec, vspec, vspec, aspec, aspec, aspec),
        scratch_shapes=scratch,
        compiler_params=pltpu.CompilerParams(
            collective_id=0, has_side_effects=True, vmem_limit_bytes=63 * 2**20
        ),
        cost_estimate=pl.CostEstimate(
            flops=9 * 2 * R * FQ * D, bytes_accessed=6 * FQ * D * 2, transcendentals=R * FQ
        ),
        name="moe_layer",
    )(tokens, cotangent, own, gate_weight[0], up_weight[0], down_weight[0])
    steps = 4
    wide = pl.BlockSpec((toks, D // steps), lambda i: (0, i))
    grads = pl.BlockSpec((FQ, D // steps), lambda i: (0, i))
    specs = (wide, wide, pl.BlockSpec(gate_prob.shape, lambda i: (0, 0)), grads, grads, grads)
    outs = pl.pallas_call(
        settle, out_shape=shapes, grid=(steps,), in_specs=list(specs), out_specs=specs, name="settle"
    )(*outs)
    mixed, token_grad, gate_grad, dwg, dwu, dwd = outs
    return mixed, token_grad, gate_grad, dwg[None], dwu[None], dwd[None]


def solution(mesh):
    rows_spec = P(("dp", "expert"), None)
    weight_spec = P("expert", "dp", None)
    return jax.shard_map(
        body,
        mesh=mesh,
        in_specs=(rows_spec,) * 4 + (P(),) + (weight_spec,) * 3,
        out_specs=(rows_spec,) * 3 + (weight_spec,) * 3,
        check_vma=False,
    )
```

time: 278 us -> 247 us (0.89)
  Pallas kernels: 264 us -> 241 us
  local copies, waits for them, and re-layouts: 13.1 us -> 2.95 us
    pallas_call x1 -> x2, Pallas kernels: 264 us -> 241 us  [the longest x1 236 us: body(): pl.pallas_call(kernel, out_shape=shapes, in_specs=[aspec, aspec, vspec, a...]
    unnamed x12 -> x3, local copies, waits for them, and re-layouts: 13.1 us -> 2.87 us
where the time goes in v2:
time: 247 us; the launch traced here: 246 us
  Pallas kernels  241 us (98%)
  local copies, waits for them, and re-layouts  2.95 us (1%)
    pallas_call x1, Pallas kernels, body(): pl.pallas_call(kernel, out_shape=shapes, in_specs=[aspec, aspec, vspec, a...  236 us
    pallas_call x1, Pallas kernels, body(): pl.pallas_call(settle, out_shape=shapes, grid=(steps,), in_specs=list(spe...  5.15 us

profile of v2, /device:TPU:1, one launch (start us, length us, event | category | flops | bytes accessed | tf_op | source)
XLA Modules:
  0.0 246.5 jit_solution(14153936773247754357)
XLA Ops:
  0.6 0.1 pad.2.clone
  0.7 0.8 copy.18
  1.5 0.8 copy.17
  2.2 1.1 select_reduce_fusion
  3.3 0.7 maximum_maximum_fusion.own_ref
  4.0 236.0 %moe_layer.1 = (bf16[16,4096]{1,0:T(8,128)(2,1)}, bf16[16,4096]{1,0:T(8,128)(2,1)}, f32[16,8]{1,0:T(8,128)}, bf16[192,4096]{1,0:T(8,128)(2,1)}, bf16[192,4096]{1,0:T(8,128)(2,1)}, /*index=5*/bf16[192,4096]{1,0:T(8,128)(2,1)}) custom-call(bf16[16,4096]{1,0:T(8,128)(2,1)} %x_hbm.1, bf16[16,4096]{1,0:T(8,128)(2,1)} %c_hbm.1, ...), custom_call_target="tpu_custom_call" | custom-call | flops 10871635968 | bytes 9437184 | tf_op jit(solution)/shard_map/moe_layer/pallas_call | solution.py:880
  240.0 5.1 %settle.1 = (bf16[16,4096]{1,0:T(8,128)(2,1)}, bf16[16,4096]{1,0:T(8,128)(2,1)}, f32[16,8]{1,0:T(8,128)}, bf16[192,4096]{1,0:T(8,128)(2,1)}, bf16[192,4096]{1,0:T(8,128)(2,1)}, /*index=5*/bf16[192,4096]{1,0:T(8,128)(2,1)}) custom-call(bf16[16,4096]{1,0:T(8,128)(2,1)} %get-tuple-element.18.refs_0_, bf16[16,4096]{1,0:T(8,128)(2,1)} %get-tuple-element.19.refs_1_, ...), custom_call_target="tpu_custom_call" | custom-call | tf_op jit(solution)/shard_map/settle/pallas_call | solution.py:898
  245.1 1.4 copy.19
  (2 shorter events, 0.0 us)

commit v3 on v2

--- a/solution.py
+++ b/solution.py
@@ -48,7 +48,7 @@
 
 
 def kernel(
-    x_hbm, c_hbm, own_ref, wg_hbm, wu_hbm, wd_hbm,
+    x_hbm, c_hbm, ids_ref, p_ref, place_ref, wg_hbm, wu_hbm, wd_hbm,
     mixed_ref, tgrad_ref, ggrad_ref, dwg_hbm, dwu_hbm, dwd_hbm,
     zbuf, zc, sbuf, sc, xr, wg, wu, wd, pb, rly, fin_a, fin_b, ybuf, yr, cs, cr, zs, zr,
     csc, zsc, xsc, xrc,
@@ -149,7 +149,19 @@
     peers += [at_x(i) for i in range(1, NX)] + [other]
     for dev in peers:
         pl.semaphore_signal(barrier, inc=1, device_id=dev, device_id_type=MESH)
-    meta[x, mine, :] = own_ref[...]
+    eye = jnp.where(iota((TOK, TOK), 0) == iota((TOK, TOK), 1), 1.0, 0.0).astype(BF16)
+    ids = nt(eye, ids_ref[...].astype(F32).astype(BF16))
+    p3 = split3(p_ref[...])
+    probs = nt(eye, p3[0]) + nt(eye, p3[1]) + nt(eye, p3[2])
+    place = place_ref[...].astype(F32)
+    lane64 = iota((TOK, place.shape[1]), 1).astype(F32)
+    lane = iota((TOK, 128), 1)
+    own = jnp.zeros((TOK, 128), F32)
+    for k in range(8):
+        slot = jnp.sum(jnp.where(ids[:, k : k + 1] == lane64, place, 0.0), axis=1, keepdims=True)
+        own = jnp.where(lane == k, slot, own)
+        own = jnp.where(lane == 8 + k, probs[:, k : k + 1], own)
+    meta[x, mine, :] = own
     loads[0].wait()
     loads[1].wait()
     pl.semaphore_wait(barrier, len(peers))
@@ -726,14 +738,16 @@
         total = gz_r[0:TOK, :]
         for i in range(1, NZ):
             total += gz_r[i * TOK : (i + 1) * TOK, :]
-        own = own_ref[...]
+        own = meta[x, mine, :]
         lanes = iota((TOK, 128), 1).astype(F32)
         lane8 = iota((TOK, 8), 1)
         res = jnp.zeros((TOK, 8), F32)
         for k in range(8):
             val = jnp.sum(jnp.where(own[:, k : k + 1] == lanes, total, 0.0), axis=1, keepdims=True)
             res = jnp.where(lane8 == k, val, res)
-        ggrad_ref[...] = res
+        eye8 = jnp.where(iota((8, 8), 0) == iota((8, 8), 1), 1.0, 0.0).astype(BF16)
+        r3 = split3(res)
+        ggrad_ref[...] = nt(eye8, r3[0]) + nt(eye8, r3[1]) + nt(eye8, r3[2])
         ge_copy().wait_send()
         for i in range(1, NZ):
             gz_copy(i).wait_send()
@@ -743,20 +757,23 @@
         def _():
             fn(k)
 
-    START = 3
+    START = 4
     for i in z_order:
         mz_copy(i).start()
-    for k in range(2):
+    for k in range(3):
         for i in z_order:
             z_copy(i, k).start()
     for i in range(1, NZ):
         arrived(meta.at[x, z_part(i)], mzss.at[i - 1], mzrs.at[i - 1], at_z(i))
     me_copy.start()
+    guarded(st_x, START + 2 + 0 * x)
+    st_b(0)
     g_acc[...] = jnp.zeros_like(g_acc)
     u_acc[...] = jnp.zeros_like(u_acc)
     d_acc[...] = jnp.zeros_like(d_acc)
     gacc[...] = jnp.zeros_like(gacc)
     arrived(meta.at[x, oth_part], mess, mers, other)
+    st_b(1)
     for i in (2, 1, 3):
         mx_copy(i).start()
     route(x, True)
@@ -774,7 +791,7 @@
         guarded(st_gy, i - 7)
         guarded(st_d, i - 5)
         guarded(st_c, i - 4)
-        guarded(st_b, i - 3)
+        guarded(st_b, i - 3, 2)
         guarded(st_e, i - 6)
         guarded(route_other, i - 4, 0, NX - 1)
         guarded(st_f, i - 7)
@@ -794,7 +811,7 @@
         guarded(st_he, k - 7)
         guarded(st_hz, k - 8)
         guarded(st_u, k - 9)
-        guarded(st_weights, k - NH - 1, 0, NH)
+        guarded(st_weights, k - NH - 4, 0, NH)
         return carry
 
     lax.fori_loop(START, N + NH + 6 + 9, step, 0)
@@ -819,9 +836,6 @@
     R = NX * ROWS
     NT = NZ * TOK
     WO, WB = len(WIDE_OUT), len(WIDE_BACK)
-    match = expert_ids[:, :, None] == jnp.arange(placement.shape[0], dtype=jnp.int32)
-    slots = jnp.sum(jnp.where(match, placement, 0), axis=2).astype(F32)
-    own = jnp.concatenate([slots, gate_prob, jnp.zeros((toks, 112), F32)], axis=1)
     dma = pltpu.SemaphoreType.DMA
     vm = pltpu.VMEM
     vspec = pl.BlockSpec(memory_space=pltpu.VMEM)
@@ -872,7 +886,7 @@
     shapes = (
         jax.ShapeDtypeStruct((toks, D), BF16),
         jax.ShapeDtypeStruct((toks, D), BF16),
-        jax.ShapeDtypeStruct(gate_prob.shape, F32),
+        jax.ShapeDtypeStruct(gate_prob.shape[::-1], F32),
         jax.ShapeDtypeStruct((FQ, D), BF16),
         jax.ShapeDtypeStruct((FQ, D), BF16),
         jax.ShapeDtypeStruct((FQ, D), BF16),
@@ -880,7 +894,7 @@
     outs = pl.pallas_call(
         kernel,
         out_shape=shapes,
-        in_specs=[aspec, aspec, vspec, aspec, aspec, aspec],
+        in_specs=[aspec, aspec, vspec, vspec, vspec, aspec, aspec, aspec],
         out_specs=(vspec, vspec, vspec, aspec, aspec, aspec),
         scratch_shapes=scratch,
         compiler_params=pltpu.CompilerParams(
@@ -890,16 +904,19 @@
             flops=9 * 2 * R * FQ * D, bytes_accessed=6 * FQ * D * 2, transcendentals=R * FQ
         ),
         name="moe_layer",
-    )(tokens, cotangent, own, gate_weight[0], up_weight[0], down_weight[0])
-    steps = 4
+    )(
+        tokens, cotangent, expert_ids.T, gate_prob.T, placement.reshape(1, -1),
+        gate_weight[0], up_weight[0], down_weight[0],
+    )
+    steps = 2
     wide = pl.BlockSpec((toks, D // steps), lambda i: (0, i))
     grads = pl.BlockSpec((FQ, D // steps), lambda i: (0, i))
-    specs = (wide, wide, pl.BlockSpec(gate_prob.shape, lambda i: (0, 0)), grads, grads, grads)
+    specs = (wide, wide, pl.BlockSpec(gate_prob.shape[::-1], lambda i: (0, 0)), grads, grads, grads)
     outs = pl.pallas_call(
         settle, out_shape=shapes, grid=(steps,), in_specs=list(specs), out_specs=specs, name="settle"
     )(*outs)
     mixed, token_grad, gate_grad, dwg, dwu, dwd = outs
-    return mixed, token_grad, gate_grad, dwg[None], dwu[None], dwd[None]
+    return mixed, token_grad, gate_grad.T, dwg[None], dwu[None], dwd[None]
 
 
 def solution(mesh):

time: 247 us -> 235 us (0.951)
  Pallas kernels: 241 us -> 233 us
  local copies, waits for them, and re-layouts: 2.95 us -> 0 us
    pallas_call x1, Pallas kernels: 236 us -> 229 us  [body(): pl.pallas_call(kernel, out_shape=shapes, in_specs=[aspec, aspec, vspec, v...]
    unnamed x3 -> x0, local copies, waits for them, and re-layouts: 2.87 us -> none
where the time goes in v3:
time: 235 us; the launch traced here: 234 us
  Pallas kernels  233 us (99%)
    pallas_call x1, Pallas kernels, body(): pl.pallas_call(kernel, out_shape=shapes, in_specs=[aspec, aspec, vspec, v...  229 us

profile of v3, /device:TPU:1, one launch (start us, length us, event | category | flops | bytes accessed | tf_op | source)
XLA Modules:
  0.0 233.8 jit_solution(16341062098286722188)
XLA Ops:
  0.6 228.7 %moe_layer.1 = (bf16[16,4096]{1,0:T(8,128)(2,1)}, bf16[16,4096]{1,0:T(8,128)(2,1)}, f32[8,16]{1,0:T(8,128)}, bf16[192,4096]{1,0:T(8,128)(2,1)}, bf16[192,4096]{1,0:T(8,128)(2,1)}, /*index=5*/bf16[192,4096]{1,0:T(8,128)(2,1)}) custom-call(bf16[16,4096]{1,0:T(8,128)(2,1)} %x_hbm.1, bf16[16,4096]{1,0:T(8,128)(2,1)} %c_hbm.1, s32[8,16]{1,0:T(8,128)} %bitcast.16, ...), custom_call_target="tpu_custom_call" | custom-call | flops 10871635968 | bytes 9437184 | tf_op jit(solution)/shard_map/moe_layer/pallas_call | solution.py:894
  229.4 4.4 %settle.1 = (bf16[16,4096]{1,0:T(8,128)(2,1)}, bf16[16,4096]{1,0:T(8,128)(2,1)}, f32[8,16]{1,0:T(8,128)}, bf16[192,4096]{1,0:T(8,128)(2,1)}, bf16[192,4096]{1,0:T(8,128)(2,1)}, /*index=5*/bf16[192,4096]{1,0:T(8,128)(2,1)}) custom-call(bf16[16,4096]{1,0:T(8,128)(2,1)} %get-tuple-element.18.refs_0_, bf16[16,4096]{1,0:T(8,128)(2,1)} %get-tuple-element.19.refs_1_, ...), custom_call_target="tpu_custom_call" | custom-call | tf_op jit(solution)/shard_map/settle/pallas_call | solution.py:915
